TPU v7x, 128 devices: a whole 4x4x4 slice. The times are simulated.
128 devices in a mesh: energy: 16 (over z, x_hi, core), momentum: 8 (over y, x_lo).
Axes of the slice: x: 4 (x_hi: 2, x_lo: 2; x = x_hi * 2 + x_lo), y: 4, z: 4, core: 2. Of those that a mesh axis runs over, the one named last changes fastest.
Arguments:
- hopping: float32 [8, 2, 2, 384, 384], P('momentum'), may hold values from -0.07 to 0.07, as said below
- coupling: float32 [8, 2, 384, 384], P('momentum'), may hold values from -0.15 to 0.15
- onsite: float32 [2, 384], replicated, may hold values from -4 to -2.5
- sigma_in: float32 [16, 8, 2, 147456], P('energy', 'momentum'), may hold values from -0.12 to 0.12
- neighbor_shift: int32 [96, 48], replicated, may hold values from 1 to 95
- mode_shift: int32 [6], replicated, may hold values from 1 to 7
- phonon_kernel: float32 [6, 2, 8, 8], replicated, may hold values from -240 to 240
Outputs:
- sigma_new: float32 [16, 8, 2, 147456], P('energy', 'momentum')
Inputs may be any that keep to these rules, and one draw needn't show every extreme that they name: hopping[k, c, 0] is symmetric with a zero diagonal and hopping[k, c, 1] is antisymmetric, so every cell block is Hermitian.
All inputs are finite; a program needn't handle non-finite values.
Results may differ from a plain program's by a relative error of at most 0.0003.
Values sent between devices are 32-bit elements; how exact they have to be, the bound alone decides.
No kernel may reach another device: no remote copies, remote signals or barrier semaphores. Data moves between devices by JAX's collectives and lax.ppermute only.
A program may use at most 256 MiB of HBM per device.

v0:
```python
import jax
import jax.numpy as jnp
from jax import lax
from jax.sharding import PartitionSpec as P

ORB = 384
ORB_ATOM = 4
ATOMS = 96
NEIGH = 48
PAIR_COLS = 147456
MODES = 6


BROADENING = 0.5


def matmul_high(first_matrix, second_matrix):
    return jnp.dot(
        first_matrix,
        second_matrix,
        precision=lax.Precision.HIGHEST,
        preferred_element_type=jnp.float32,
    )


def complex_product(first_pair, second_pair):
    real_real = matmul_high(first_pair[0], second_pair[0])
    imag_imag = matmul_high(first_pair[1], second_pair[1])
    summed = matmul_high(first_pair[0] + first_pair[1], second_pair[0] + second_pair[1])
    return (real_real - imag_imag, summed - real_real - imag_imag)


def newton_inverse(system):
    diagonal_real = jnp.diagonal(system[0])
    diagonal_imag = jnp.diagonal(system[1])
    magnitude = diagonal_real * diagonal_real + diagonal_imag * diagonal_imag
    inverse_real = diagonal_real / magnitude
    inverse_imag = -diagonal_imag / magnitude
    column_real = system[0] * inverse_real[None, :] - system[1] * inverse_imag[None, :]
    column_imag = system[0] * inverse_imag[None, :] + system[1] * inverse_real[None, :]
    scaled_real = inverse_real[:, None] * column_real - inverse_imag[:, None] * column_imag
    scaled_imag = inverse_real[:, None] * column_imag + inverse_imag[:, None] * column_real
    guess = (2.0 * jnp.diag(inverse_real) - scaled_real, 2.0 * jnp.diag(inverse_imag) - scaled_imag)
    product = complex_product(system, guess)
    correction = complex_product(guess, product)
    guess = (2.0 * guess[0] - correction[0], 2.0 * guess[1] - correction[1])
    return guess


def place_pairs(pair_values, row_atom, col_atom):
    entries = pair_values.reshape(ATOMS, NEIGH, 2, ORB_ATOM, ORB_ATOM)
    placed = (
        jnp.zeros((2, ATOMS, ORB_ATOM, ATOMS, ORB_ATOM), jnp.float32)
        .at[:, row_atom, :, col_atom, :]
        .add(entries)
    )
    placed = placed.reshape(2, ORB, ORB)
    return (placed[0], placed[1])


def pick_pairs(matrix_pair, row_atom, col_atom):
    stacked = jnp.stack([matrix_pair[0], matrix_pair[1]]).reshape(
        2, ATOMS, ORB_ATOM, ATOMS, ORB_ATOM
    )
    return stacked[:, row_atom, :, col_atom, :].reshape(PAIR_COLS)


def green_point(
    energy_real, hopping_block, coupling_block, onsite, sigma_point, row_atom, col_atom
):
    identity = jnp.eye(ORB, dtype=jnp.float32)
    systems = []
    for cell_index in range(2):
        self_energy = place_pairs(sigma_point[cell_index], row_atom, col_atom)
        system_real = (
            jnp.diag(energy_real - onsite[cell_index])
            - hopping_block[cell_index, 0]
            - self_energy[0]
        )
        system_imag = BROADENING * identity - hopping_block[cell_index, 1] - self_energy[1]
        systems.append((system_real, system_imag))
    first_green = newton_inverse(systems[0])
    coupling_pair = (coupling_block[0], coupling_block[1])
    coupling_adjoint = (coupling_block[0].T, -coupling_block[1].T)
    adjoint_green = complex_product(coupling_adjoint, first_green)
    folded = complex_product(adjoint_green, coupling_pair)
    second_green = newton_inverse((systems[1][0] - folded[0], systems[1][1] - folded[1]))
    green_coupling = complex_product(first_green, coupling_pair)
    through = complex_product(complex_product(green_coupling, second_green), adjoint_green)
    first_full = (first_green[0] + through[0], first_green[1] + through[1])
    return jnp.stack(
        [pick_pairs(first_full, row_atom, col_atom), pick_pairs(second_green, row_atom, col_atom)]
    )


def build_kernel(mode_shift, phonon_kernel, energies, momenta):
    target = lax.broadcasted_iota(jnp.int32, (MODES, energies, energies), 1)
    source = lax.broadcasted_iota(jnp.int32, (MODES, energies, energies), 2)
    shifted = mode_shift[:, None, None]
    lower = (source == target - shifted).astype(jnp.float32)
    upper = (source == target + shifted).astype(jnp.float32)
    combined = jnp.einsum(
        "jab,jkq->akbq", lower, phonon_kernel[:, 0], precision=lax.Precision.HIGHEST
    )
    combined = combined + jnp.einsum(
        "jab,jkq->akbq", upper, phonon_kernel[:, 1], precision=lax.Precision.HIGHEST
    )
    return combined.reshape(energies * momenta, energies * momenta)


def body(hopping, coupling, onsite, sigma_in, neighbor_shift, mode_shift, phonon_kernel):
    local_energies = sigma_in.shape[0]
    local_momenta = sigma_in.shape[1]
    energy_devices = lax.axis_size("energy")
    momentum_devices = lax.axis_size("momentum")
    device_count = energy_devices * momentum_devices
    energies = local_energies * energy_devices
    momenta = local_momenta * momentum_devices
    owned_cols = PAIR_COLS // device_count
    row_atom = lax.broadcasted_iota(jnp.int32, (ATOMS, NEIGH), 0)
    col_atom = (row_atom + neighbor_shift) % ATOMS
    first_energy = lax.axis_index("energy") * local_energies
    energy_real = 2.0 * ((first_energy + 0).astype(jnp.float32) + 0.5) / energies
    blocks = [
        green_point(
            energy_real, hopping[0], coupling[0], onsite, sigma_in[0, 0], row_atom, col_atom
        )
    ]
    green_pairs = jnp.stack(blocks).reshape(
        1, 1, local_energies, local_momenta, 2, device_count, owned_cols
    )
    points = energies * momenta
    kernel = build_kernel(mode_shift, phonon_kernel, energies, momenta)
    kernel = kernel.reshape(
        energy_devices,
        local_energies,
        momentum_devices,
        local_momenta,
        energy_devices,
        local_energies,
        momentum_devices,
        local_momenta,
    )
    kernel = kernel.transpose(0, 2, 1, 3, 4, 6, 5, 7).reshape(points, points)
    received = lax.all_to_all(
        green_pairs, ("energy", "momentum"), split_axis=5, concat_axis=0, tiled=True
    )
    array_shape = received.shape
    flattened = received.reshape(points, -1)
    convolved = matmul_high(kernel, flattened).reshape(array_shape)
    returned = lax.all_to_all(
        convolved, ("energy", "momentum"), split_axis=0, concat_axis=5, tiled=True
    )
    return returned.reshape(local_energies, local_momenta, 2, PAIR_COLS)


def solution(mesh):
    return jax.shard_map(
        body,
        mesh=mesh,
        in_specs=(
            P("momentum", None, None, None, None),
            P("momentum", None, None, None),
            P(),
            P("energy", "momentum", None, None),
            P(),
            P(),
            P(),
        ),
        out_specs=P("energy", "momentum", None, None),
        check_vma=False,
    )
```

profile of v0, /device:TPU:1, one launch (start us, length us, event | category | flops | bytes accessed | tf_op | source)
XLA Modules:
  0.0 2081.7 jit_solution(1439246674767785035)
XLA Ops:
  10.3 25.8 %reshape.486 = f32[4608,2,4,4]{3,2,1,0:T(4,128)} reshape(f32[147456]{0:T(1024)S(1)} %get-tuple-element.6) | data formatting | bytes 1179648 | tf_op jit(solution)/shard_map/reshape;squeeze | solution.py:51
  36.1 12.4 broadcast.413.clone
  48.5 508.8 %scatter_fusion = f32[9216,2,4,4]{3,2,1,0:T(4,128)} fusion(f32[9216,2,4,4]{3,2,1,0:T(4,128)} %broadcast.413.clone, s32[4608]{0:T(1024)S(1)} %reshape.484, f32[4608,2,4,4]{3,2,1,0:T(4,128)} %reshape.486), kind=kCustom, calls=%fused_computation.6 | custom fusion | flops 147456 | bytes 1787904
  557.3 24.7 %copy.168 = f32[96,96,2,4,4]{1,0,4,3,2:T(8,128)S(1)} copy(f32[96,96,2,4,4]{4,3,2,1,0:T(4,128)} %bitcast.155) | data formatting | bytes 2359296
  582.1 9.5 copy.137
  591.7 17.6 squeeze.53
  609.3 9.5 copy.138
  618.8 17.6 squeeze.55
  648.7 21.8 %squeeze.56 = f32[1,96,4,96,4]{4,3,2,1,0:T(8,128)} reshape(f32[1,1,384,384]{3,2,1,0:T(8,128)} %get-tuple-element.17) | data formatting | bytes 1179648 | tf_op jit(solution)/shard_map/squeeze | solution.py:77
  670.5 11.6 copy.140
  682.1 20.9 %squeeze.57 = f32[1,96,4,96,4]{4,3,2,1,0:T(8,128)} reshape(f32[1,1,384,384]{3,2,1,0:T(8,128)S(1)} %get-tuple-element.16) | data formatting | bytes 1179648 | tf_op jit(solution)/shard_map/squeeze | solution.py:80
  703.0 11.6 copy.146
  718.5 10.8 copy.141
  729.4 9.5 copy.149
  748.4 17.6 add.201
  766.0 17.1 sub.263
  783.1 9.6 copy.148
  792.7 17.2 sub.269
  809.8 17.7 sub.270
  827.6 9.5 copy.150
  837.1 17.7 sub.272
  854.8 9.5 copy.152
  864.3 18.1 add.203
  900.6 25.8 %reshape.492 = f32[4608,2,4,4]{3,2,1,0:T(4,128)} reshape(f32[147456]{0:T(1024)S(1)} %copy-done.21) | data formatting | bytes 1179648 | tf_op jit(solution)/shard_map/reshape;squeeze | solution.py:51
  926.4 12.4 broadcast.413.clone.1
  938.8 508.8 %scatter_fusion.1 = f32[9216,2,4,4]{3,2,1,0:T(4,128)} fusion(f32[9216,2,4,4]{3,2,1,0:T(4,128)} %broadcast.413.clone.1, s32[4608]{0:T(1024)S(1)} %copy-done.31, f32[4608,2,4,4]{3,2,1,0:T(4,128)} %reshape.492), kind=kCustom, calls=%fused_computation.7 | custom fusion | flops 147456 | bytes 1787904
  1447.6 25.7 %copy.169 = f32[96,96,2,4,4]{1,0,4,3,2:T(8,128)} copy(f32[96,96,2,4,4]{4,3,2,1,0:T(4,128)} %bitcast.154) | data formatting | bytes 2359296
  1475.9 10.6 copy.154
  1486.5 17.6 squeeze.61
  1504.1 10.6 copy.156
  1514.8 17.6 squeeze.63
  1561.8 21.8 %stack.29 = f32[1,96,4,96,4]{4,3,2,1,0:T(8,128)} reshape(f32[384,384]{1,0:T(8,128)} %copy-done.15) | data formatting | bytes 1179648 | tf_op jit(solution)/shard_map/stack | solution.py:62
  1587.8 21.9 %stack.30 = f32[1,96,4,96,4]{4,3,2,1,0:T(8,128)} reshape(f32[384,384]{1,0:T(8,128)} %fusion.9) | data formatting | bytes 1179648 | tf_op jit(solution)/shard_map/stack | solution.py:62
  1619.7 20.9 %stack.26 = f32[1,96,4,96,4]{4,3,2,1,0:T(8,128)} reshape(f32[384,384]{1,0:T(8,128)S(1)} %fusion.12) | data formatting | bytes 1179648 | tf_op jit(solution)/shard_map/stack | solution.py:62
  1640.6 23.5 %copy.158 = f32[1,96,4,96,4]{4,2,3,1,0:T(4,128)} copy(f32[1,96,4,96,4]{4,3,2,1,0:T(8,128)} %stack.26) | data formatting | bytes 1179648 | tf_op jit(solution)/shard_map/stack | solution.py:62
  1664.1 20.9 %stack.25 = f32[1,96,4,96,4]{4,3,2,1,0:T(8,128)} reshape(f32[384,384]{1,0:T(8,128)S(1)} %copy-done.23) | data formatting | bytes 1179648 | tf_op jit(solution)/shard_map/stack | solution.py:62
  1685.0 23.8 %copy.157 = f32[1,96,4,96,4]{4,2,3,1,0:T(4,128)} copy(f32[1,96,4,96,4]{4,3,2,1,0:T(8,128)} %stack.25) | data formatting | bytes 1179648 | tf_op jit(solution)/shard_map/stack | solution.py:62
  1709.0 25.9 %pad_maximum_fusion = f32[2,96,4,96,4]{4,2,3,1,0:T(4,128)} fusion(f32[1,96,4,96,4]{4,2,3,1,0:T(4,128)} %copy.158, f32[1,96,4,96,4]{4,2,3,1,0:T(4,128)} %copy.157), kind=kLoop, calls=%fused_computation.8 | loop fusion | flops 294912 | bytes 2359296 | tf_op jit(solution)/shard_map/stack | solution.py:62
  1734.8 83.0 %gather_fusion.4 = f32[4608,2,4,4]{3,2,1,0:T(4,128)} fusion(f32[2,96,4,96,4]{4,2,3,1,0:T(4,128)} %pad_maximum_fusion, s32[4608]{0:T(1024)S(1)} %reshape.472), kind=kCustom, calls=%fused_computation.4 | custom fusion | bytes 1216512 | tf_op jit(solution)/shard_map/gather | solution.py:65
  1817.8 23.1 %stack.28 = f32[1,1,1,1,1,128,1152]{6,5,4,3,2,1,0:T(8,128)S(1)} reshape(f32[4608,2,4,4]{3,2,1,0:T(4,128)} %gather_fusion.4) | data formatting | bytes 1179648 | tf_op jit(solution)/shard_map/stack | solution.py:91
  1840.9 23.5 %copy.161 = f32[1,96,4,96,4]{4,2,3,1,0:T(4,128)} copy(f32[1,96,4,96,4]{4,3,2,1,0:T(8,128)} %stack.30) | data formatting | bytes 1179648 | tf_op jit(solution)/shard_map/stack | solution.py:62
  1864.4 23.4 %copy.160 = f32[1,96,4,96,4]{4,2,3,1,0:T(4,128)} copy(f32[1,96,4,96,4]{4,3,2,1,0:T(8,128)} %stack.29) | data formatting | bytes 1179648 | tf_op jit(solution)/shard_map/stack | solution.py:62
  1887.8 25.8 %pad_maximum_fusion.1 = f32[2,96,4,96,4]{4,2,3,1,0:T(4,128)} fusion(f32[1,96,4,96,4]{4,2,3,1,0:T(4,128)} %copy.161, f32[1,96,4,96,4]{4,2,3,1,0:T(4,128)} %copy.160), kind=kLoop, calls=%fused_computation.9 | loop fusion | flops 294912 | bytes 2359296 | tf_op jit(solution)/shard_map/stack | solution.py:62
  1913.6 82.5 %gather_fusion.5 = f32[4608,2,4,4]{3,2,1,0:T(4,128)} fusion(f32[2,96,4,96,4]{4,2,3,1,0:T(4,128)} %pad_maximum_fusion.1, s32[4608]{0:T(1024)S(1)} %reshape.472), kind=kCustom, calls=%fused_computation.5 | custom fusion | bytes 1216512 | tf_op jit(solution)/shard_map/gather | solution.py:65
  1996.1 23.2 %stack.32 = f32[1,1,1,1,1,128,1152]{6,5,4,3,2,1,0:T(8,128)S(1)} reshape(f32[4608,2,4,4]{3,2,1,0:T(4,128)} %gather_fusion.5) | data formatting | bytes 1179648 | tf_op jit(solution)/shard_map/stack | solution.py:91
  2021.4 11.5 all-to-all-start
  2034.8 18.3 all-to-all-done
  2055.9 24.6 %all_to_all.30 = f32[128,1,1,1,2,1,1152]{6,4,5,3,2,1,0:T(2,128)S(1)} all-to-all(f32[128,1,1,1,2,1,1152]{6,4,5,3,2,1,0:T(2,128)S(1)} %copy.164), channel_id=1, replica_groups=mesh['energy'=16,'momentum'=8] {'energy','momentum'}, dimensions={0} | all-to-all | bytes 2359296 | tf_op jit(solution)/shard_map/all_to_all | solution.py:151
  (155 shorter events, 107.9 us)
Async XLA Ops:
  0.0 644.5 %copy-start = (s32[384]{0:T(512)}, s32[384]{0:T(512)S(1)}, u32[]{:S(2)}) copy-start(s32[384]{0:T(512)S(1)} %or_reduce_fusion) | copy-start | bytes 4612
  1.8 46.7 %copy-start.30 = (s32[4608]{0:T(1024)}, s32[4608]{0:T(1024)S(1)}, u32[]{:S(2)}) copy-start(s32[4608]{0:T(1024)S(1)} %reshape.484) | copy-start | bytes 55300
  636.5 2.1 copy-start.37
  718.5 10.8 copy-start.7
  766.0 17.1 copy-start.19
  809.8 17.7 copy-start.18
  837.1 17.7 copy-start.17
  864.3 19.4 copy-start.20
  882.4 3.9 copy-start.22
  882.4 3.9 copy-start.24
  890.5 1.8 copy-start.2
  895.0 5.6 copy-start.21
  897.6 0.8 copy-start.13
  897.6 634.8 %copy-start.11 = (f32[384,384]{0,1:T(8,128)}, f32[384,384]{0,1:T(8,128)S(1)}, u32[]{:S(2)}) copy-start(f32[384,384]{0,1:T(8,128)S(1)} %get-tuple-element.10) | copy-start | bytes 1769476
  926.4 12.4 copy-start.31
  1514.8 17.6 copy-start.36
  1532.4 3.0 copy-start.9
  1532.4 3.0 copy-start.16
  1532.4 3.0 copy-start.25
  1535.4 2.5 copy-start.1
  1546.8 8.8 copy-start.26
  1548.3 7.3 copy-start.28
  1548.3 2.6 copy-start.33
  1549.6 10.7 copy-start.3
  1550.9 9.4 copy-start.5
  1553.3 0.8 copy-start.29
  1555.6 2.5 copy-start.32
  1558.1 2.1 copy-start.15
  1561.8 21.8 %copy-start.27 = (f32[384,384]{1,0:T(8,128)S(1)}, f32[384,384]{1,0:T(8,128)}, u32[]{:S(2)}) copy-start(f32[384,384]{1,0:T(8,128)} %copy-done.26) | copy-start | bytes 1769476
  1587.8 21.9 %copy-start.8 = (f32[384,384]{1,0:T(8,128)S(1)}, f32[384,384]{1,0:T(8,128)}, u32[]{:S(2)}) copy-start(f32[384,384]{1,0:T(8,128)} %fusion.9) | copy-start | bytes 1769476
  1587.8 24.3 %copy-start.4 = (f32[384,384]{1,0:T(8,128)S(1)}, f32[384,384]{1,0:T(8,128)}, u32[]{:S(2)}) copy-start(f32[384,384]{1,0:T(8,128)} %copy-done.3) | copy-start | bytes 1769476
  1587.8 24.3 %copy-start.6 = (f32[384,384]{1,0:T(8,128)S(1)}, f32[384,384]{1,0:T(8,128)}, u32[]{:S(2)}) copy-start(f32[384,384]{1,0:T(8,128)} %copy-done.5) | copy-start | bytes 1769476
  1612.1 2.9 copy-start.14
  1612.1 4.1 copy-start.12
  1616.2 2.1 copy-start.10
  1640.6 23.5 %copy-start.23 = (f32[384,384]{1,0:T(8,128)S(1)}, f32[384,384]{1,0:T(8,128)}, u32[]{:S(2)}) copy-start(f32[384,384]{1,0:T(8,128)} %get-tuple-element.41) | copy-start | bytes 1769476
  1685.0 23.8 %copy-start.34 = (s32[96,48,1]{0,1,2:T(8,128)S(1)}, s32[96,48,1]{0,1,2:T(8,128)}, u32[]{:S(2)}) copy-start(s32[96,48,1]{0,1,2:T(8,128)} %shift-left_or_fusion) | copy-start | bytes 55300
  2019.4 13.4 copy-start.35
  2019.4 13.7 copy-start.38
  2021.4 31.8 %all-to-all-start = ((f32[1,1,1,1,2,128,1152]{6,4,3,2,1,0,5:T(2,128)}), f32[1,1,1,1,2,128,1152]{6,4,3,2,1,0,5:T(2,128)S(1)}, u32[]{:S(2)}, u32[]{:S(2)}) async-start(f32[1,1,1,1,2,128,1152]{6,4,3,2,1,0,5:T(2,128)} %copy.162), calls=%async_computation | async-start | bytes 2359296 | tf_op jit(solution)/shard_map/all_to_all | solution.py:145
where the time goes:
time: 2120 us; the launch traced here: 2080 us
  other arithmetic  1080 us (51%)
  local copies, waits for them, and re-layouts  895 us (42%)
  matrix products  53.3 us (3%)
  blocking collectives  24.6 us (1%)
    unnamed x5, other arithmetic  1020 us
    another operation x8, local copies, waits for them, and re-layouts, pick_pairs(): jnp.stack([matrix_pair[0], matrix_pair[1]])  180 us
    gather x2, local copies, waits for them, and re-layouts, pick_pairs(): return stacked[:, row_atom, :, col_atom, :].reshape(PAIR_COLS)  166 us
    unnamed x87, local copies, waits for them, and re-layouts  78.4 us
    squeeze x4, local copies, waits for them, and re-layouts, place_pairs(): return (placed[0], placed[1])  70.6 us
    dot_general x28, matrix products, matmul_high(): jnp.dot(first_matrix, second_matrix, precision=lax.Precision.HIGHEST, pre...  52.5 us
    another operation x2, other arithmetic, pick_pairs(): jnp.stack([matrix_pair[0], matrix_pair[1]])  51.7 us
    another operation x2, local copies, waits for them, and re-layouts, place_pairs(): entries = pair_values.reshape(ATOMS, NEIGH, 2, ORB_ATOM, ORB_ATOM)  51.5 us
  transfers between devices with their start and end apart: 1, of which 1 were waited for; matrix products, arithmetic and copies ran while one was open for 0% of the time, Pallas kernels for 0%

commit v1 on v0

v1 whole, which is shorter than its diff:
```python
import jax
import jax.numpy as jnp
from jax import lax
from jax.experimental import pallas as pl
from jax.experimental.pallas import tpu as pltpu
from jax.sharding import PartitionSpec as P

ORB = 384
ATOMS = 96
NEIGH = 48
PAIR_COLS = 147456
MODES = 6
BROADENING = 0.5
BLOCKS = ATOMS // 8
ROWS = 2 * PAIR_COLS // 128
STRIP = 32
DUO = 2 * ORB
NONE = 64

F32 = jnp.float32
BF16 = jnp.bfloat16


def lanes(table, index):
    return jnp.take_along_axis(table, index, axis=1, mode="promise_in_bounds")


def iota(dim):
    return lax.broadcasted_iota(jnp.int32, (8, 128), dim)


def pair_row(cell, block, orbital, part):
    return pl.multiple_of((((cell * BLOCKS + block) * 4 + orbital) * 3 + part) * 8, 8)


def split_store(value, hi_ref, lo_ref, rows, cols):
    hi = value.astype(BF16)
    hi_ref[rows, cols] = hi
    lo_ref[rows, cols] = (value - hi.astype(F32)).astype(BF16)


def store_left(pair, left, row):
    rows = pl.ds(row, STRIP)
    for t in range(2):
        split_store(pair[t], left[0], left[1], rows, slice(t * ORB, (t + 1) * ORB))


def store_right(pair, right, row):
    upper, lower = pl.ds(row, STRIP), pl.ds(pl.multiple_of(row + ORB, STRIP), STRIP)
    real, imag = slice(0, ORB), slice(ORB, DUO)
    split_store(pair[0], right[0], right[1], upper, real)
    split_store(pair[0], right[0], right[1], lower, imag)
    split_store(pair[1], right[0], right[1], upper, imag)
    split_store(-pair[1], right[0], right[1], lower, real)


def product(left, right, out):
    for col in range(0, DUO, 256):
        cols = slice(col, col + 256)
        total = jnp.dot(left[0][...], right[0][:, cols], preferred_element_type=F32)
        total = total + jnp.dot(left[1][...], right[0][:, cols], preferred_element_type=F32)
        total = total + jnp.dot(left[0][...], right[1][:, cols], preferred_element_type=F32)
        out[:, cols] = total


def strips(step):
    def one(index, carry):
        step(pl.multiple_of(index * STRIP, STRIP))
        return carry

    lax.fori_loop(0, ORB // STRIP, one, 0)


def load_pair(ref, row):
    rows = pl.ds(row, STRIP)
    return ref[rows, 0:ORB], ref[rows, ORB:DUO]


def index_tables(shift_ref, block):
    lane = iota(1)
    atom = iota(0) + 8 * block
    col = atom + shift_ref[pl.ds(pl.multiple_of(8 * block, 8), 8), :]
    col = jnp.where(col >= ATOMS, col - ATOMS, col)
    following = jnp.full((8, 128), NONE, jnp.int32)
    first = jnp.full((8, 128), NONE, jnp.int32)
    for n in range(NEIGH - 1, -1, -1):
        here = jnp.broadcast_to(col[:, n : n + 1], (8, 128))
        following = jnp.where((col == here) & (lane < n), n, following)
        first = jnp.where(lane == here, n, first)
    return col, following, first


def unshuffle_in(sigma_ref, cell, block):
    lane = iota(1)
    group = lane // 16
    inner = (lane // 4) % 4
    orbital_j = lane % 4
    natural = [
        sigma_ref[pl.ds(block * 8 * 24 + g * 2 + cell, 8, stride=24), :] for g in range(12)
    ]
    out = []
    for i in range(4):
        for u in range(3):
            if u < 2:
                index = inner * 32 + 16 * u + 4 * i + orbital_j
                sources = range(8)
                pick = group
            else:
                index = inner * 32 + 16 * (lane // 64) + 4 * i + orbital_j
                sources = range(8, 12)
                pick = group % 4 + 8
            value = lanes(natural[sources[0]], index)
            for g in sources[1:]:
                value = jnp.where(pick == g, lanes(natural[g], index), value)
            out.append(value)
    return out


def place_block(shift_ref, sigma_ref, system, pair_ref, chain_ref, table_ref, block):
    lane = iota(1)
    quarter = lane // 4
    orbital_j = lane % 4
    late = 32 + (lane % 64) // 4
    half = lane // 64
    col, following, first = index_tables(shift_ref, block)
    rows8 = pl.ds(pl.multiple_of(8 * block, 8), 8)
    table_ref[0, rows8, :] = lanes(col, quarter)
    table_ref[1, rows8, :] = lanes(col, late)
    for cell in range(2):
        for slot, value in enumerate(unshuffle_in(sigma_ref, cell, block)):
            pair_ref[cell * 12 + slot] = value
    chain_ref[...] = following

    def more(least):
        return least < NEIGH

    def join(least):
        chain = chain_ref[...]
        early_next = lanes(chain, quarter)
        late_next = lanes(chain, late)
        low = (4 * early_next + orbital_j) % 128
        high = (4 * early_next + orbital_j) % 64
        last = 64 * half + (4 * late_next + orbital_j) % 64
        for base in range(0, 24, 3):
            tail = pair_ref[base + 2]
            for t in range(2):
                value = pair_ref[base + t]
                added = jnp.where(
                    early_next < 32,
                    lanes(value, low),
                    jnp.where(early_next < NEIGH, lanes(tail, high + 64 * t), 0.0),
                )
                pair_ref[base + t] = value + added
            pair_ref[base + 2] = tail + jnp.where(late_next < NEIGH, lanes(tail, last), 0.0)
        chain = lanes(chain, chain)
        chain_ref[...] = chain
        return jnp.min(chain)

    lax.while_loop(more, join, jnp.min(following))
    for v in range(3):
        entry = lanes(first, 32 * v + quarter)
        low = (4 * entry + orbital_j) % 128
        high = (4 * entry + orbital_j) % 64
        for cell in range(2):
            for i in range(4):
                base = cell * 12 + i * 3
                rows = pl.ds(32 * block + i, 8, stride=4)
                tail = pair_ref[base + 2]
                for t in range(2):
                    value = jnp.where(
                        entry < 32,
                        lanes(pair_ref[base + t], low),
                        jnp.where(entry < NEIGH, lanes(tail, high + 64 * t), 0.0),
                    )
                    system[cell][3 * t + v, rows, :] -= value


def pick_block(green, table_ref, out_ref, cell, block):
    lane = iota(1)
    orbital_j = lane % 4
    rows8 = pl.ds(pl.multiple_of(8 * block, 8), 8)
    early = table_ref[0, rows8, :]
    late = table_ref[1, rows8, :]
    for i in range(4):
        rows = pl.ds(32 * block + i, 8, stride=4)
        source = [green[s, rows, :] for s in range(6)]
        for u in range(3):
            col = early if u < 2 else late
            index = (4 * col + orbital_j) % 128
            chosen = col // 32
            options = source[3 * u : 3 * u + 3] if u < 2 else source
            if u == 2:
                chosen = chosen + 3 * (lane // 64)
            value = lanes(options[0], index)
            for s in range(1, len(options)):
                value = jnp.where(chosen == s, lanes(options[s], index), value)
            out_ref[pl.ds(pair_row(cell, block, i, u), 8), :] = value


def block_loop(step):
    def one(block, carry):
        step(block)
        return carry

    lax.fori_loop(0, BLOCKS, one, 0)


def load_tiles(ref, row):
    rows = pl.ds(row, STRIP)
    return tuple(
        jnp.concatenate([ref[3 * t + v, rows, :] for v in range(3)], axis=1) for t in range(2)
    )


def store_tiles(pair, ref, row):
    rows = pl.ds(row, STRIP)
    for t in range(2):
        for v in range(3):
            ref[3 * t + v, rows, :] = pair[t][:, 128 * v : 128 * (v + 1)]


def diagonal_mask(row):
    at = lax.broadcasted_iota(jnp.int32, (STRIP, ORB), 0) + row
    return at == lax.broadcasted_iota(jnp.int32, (STRIP, ORB), 1)


def inverse_into(shift, onsite_row, system, fold, diag_ref, col_ref, temp, green, left, right, square):
    diag_ref[...] = jnp.zeros_like(diag_ref)

    def full(row):
        real, imag = load_tiles(system, row)
        mask = diagonal_mask(row)
        real = real + jnp.where(mask, shift - onsite_row, 0.0)
        imag = imag + jnp.where(mask, BROADENING, 0.0)
        if fold is not None:
            fold_real, fold_imag = load_pair(fold, row)
            real, imag = real - fold_real, imag - fold_imag
        return real, imag, mask

    def diagonal(row):
        real, imag, mask = full(row)
        real, imag = jnp.where(mask, real, 0.0), jnp.where(mask, imag, 0.0)
        diag_ref[0:1, :] += jnp.sum(real, axis=0, keepdims=True)
        diag_ref[1:2, :] += jnp.sum(imag, axis=0, keepdims=True)
        down_real = jnp.sum(real, axis=1, keepdims=True)
        down_imag = jnp.sum(imag, axis=1, keepdims=True)
        scale = 1.0 / (down_real * down_real + down_imag * down_imag)
        rows = pl.ds(row, STRIP)
        col_ref[0, rows, :] = jnp.broadcast_to(down_real * scale, (STRIP, 128))
        col_ref[1, rows, :] = jnp.broadcast_to(-down_imag * scale, (STRIP, 128))

    strips(diagonal)
    diag_real, diag_imag = diag_ref[0:1, :], diag_ref[1:2, :]
    scale = 1.0 / (diag_real * diag_real + diag_imag * diag_imag)
    inverse_real, inverse_imag = diag_real * scale, -diag_imag * scale

    def scaled(row):
        real, imag, mask = full(row)
        real, imag = jnp.where(mask, 0.0, real), jnp.where(mask, 0.0, imag)
        pair = (
            real * inverse_real - imag * inverse_imag,
            real * inverse_imag + imag * inverse_real,
        )
        store_tiles(pair, system, row)
        store_left(pair, left, row)
        store_right(pair, right, row)

    strips(scaled)
    product(left, right, square)
    strips(lambda row: store_right(load_pair(square, row), right, row))
    product(left, right, temp)

    def finish(row):
        first_real, first_imag = load_tiles(system, row)
        second_real, second_imag = load_pair(square, row)
        third_real, third_imag = load_pair(temp, row)
        real = jnp.where(diagonal_mask(row), 1.0, 0.0) - first_real + second_real - third_real
        imag = second_imag - first_imag - third_imag
        rows = pl.ds(row, STRIP)
        down_real, down_imag = col_ref[0, rows, 0:1], col_ref[1, rows, 0:1]
        pair = (down_real * real - down_imag * imag, down_real * imag + down_imag * real)
        store_tiles(pair, green, row)
        return pair

    return finish


def green_kernel(
    energy_ref,
    shift_in_ref,
    onsite_ref,
    sigma_ref,
    hop_ref,
    coup_ref,
    out_ref,
    shift_ref,
    table_ref,
    pair_ref,
    chain_ref,
    diag_ref,
    col_ref,
    first_system,
    second_system,
    green,
    temp,
    square,
    *operands,
):
    duos = [(operands[2 * s], operands[2 * s + 1]) for s in range(len(operands) // 2)]
    left_a, left_b, left_v, right_a, right_b, right_v = duos
    shift_ref[...] = jnp.zeros_like(shift_ref)
    shift_ref[:, 0:NEIGH] = shift_in_ref[...]
    system = (first_system, second_system)
    for cell in range(2):
        strips(
            lambda row: store_tiles(
                tuple(-hop_ref[2 * cell + t, pl.ds(row, STRIP), :] for t in range(2)), system[cell], row
            )
        )
    block_loop(
        lambda block: place_block(
            shift_ref, sigma_ref, system, pair_ref, chain_ref, table_ref, block
        )
    )
    strips(lambda row: store_right((coup_ref[0, pl.ds(row, STRIP), :], coup_ref[1, pl.ds(row, STRIP), :]), right_v, row))
    for t in range(2):
        square[:, t * ORB : (t + 1) * ORB] = coup_ref[t].T if t == 0 else -coup_ref[t].T
    strips(lambda row: store_left(load_pair(square, row), left_v, row))
    energy = energy_ref[0]

    finish = inverse_into(
        energy, onsite_ref[0:1, :], first_system, None, diag_ref, col_ref, temp, green, left_a, right_a, square
    )

    def first_done(row):
        pair = finish(row)
        store_left(pair, left_a, row)
        store_right(pair, right_a, row)

    strips(first_done)
    product(left_v, right_a, temp)

    def adjoint_done(row):
        pair = load_pair(temp, row)
        store_left(pair, left_b, row)
        store_right(pair, right_b, row)

    strips(adjoint_done)
    product(left_b, right_v, temp)
    product(left_a, right_v, square)
    strips(lambda row: store_left(load_pair(square, row), left_v, row))
    finish = inverse_into(
        energy, onsite_ref[1:2, :], second_system, temp, diag_ref, col_ref, temp, first_system, left_a, right_a, square
    )
    strips(lambda row: store_right(finish(row), right_a, row))
    block_loop(lambda block: pick_block(first_system, table_ref, out_ref, 1, block))
    product(left_v, right_a, temp)
    strips(lambda row: store_left(load_pair(temp, row), left_b, row))
    product(left_b, right_b, temp)

    def total(row):
        base = load_tiles(green, row)
        added = load_pair(temp, row)
        store_tiles((base[0] + added[0], base[1] + added[1]), green, row)

    strips(total)
    block_loop(lambda block: pick_block(green, table_ref, out_ref, 0, block))


def vmem():
    return pl.BlockSpec(memory_space=pltpu.VMEM)


def smem():
    return pl.BlockSpec(memory_space=pltpu.SMEM)


def green_pairs(energy, neighbor_shift, onsite, sigma_rows, hopping, coupling):
    left = [pltpu.VMEM((ORB, DUO), BF16)] * 2
    right = [pltpu.VMEM((DUO, DUO), BF16)] * 2
    return pl.pallas_call(
        green_kernel,
        out_shape=jax.ShapeDtypeStruct((ROWS, 128), F32),
        in_specs=[smem()] + [vmem()] * 5,
        out_specs=vmem(),
        scratch_shapes=[
            pltpu.VMEM((ATOMS, 128), jnp.int32),
            pltpu.VMEM((2, ATOMS, 128), jnp.int32),
            pltpu.VMEM((24, 8, 128), F32),
            pltpu.VMEM((8, 128), jnp.int32),
            pltpu.VMEM((8, ORB), F32),
            pltpu.VMEM((2, ORB, 128), F32),
            pltpu.VMEM((6, ORB, 128), F32),
            pltpu.VMEM((6, ORB, 128), F32),
            pltpu.VMEM((6, ORB, 128), F32),
            pltpu.VMEM((ORB, DUO), F32),
            pltpu.VMEM((ORB, DUO), F32),
            *left,
            *left,
            *left,
            *right,
            *right,
            *right,
        ],
        compiler_params=pltpu.CompilerParams(vmem_limit_bytes=56 * 2**20),
        name="green_pairs",
    )(energy, neighbor_shift, onsite, sigma_rows, hopping, coupling)


def convolve_kernel(shift_ref, phonon_ref, in_ref, out_ref):
    source_energy = iota(1) // 8
    momentum = iota(1) % 8
    tiles = []
    for m in range(MODES):
        pair = []
        for d in range(2):
            wide = jnp.concatenate([phonon_ref[m, d]] * 16, axis=1)
            pair.append(wide)
        tiles.append(pair)
    rows = []
    for energy in range(16):
        value = jnp.zeros((8, 128), F32)
        for m in range(MODES):
            value = value + jnp.where(source_energy == energy - shift_ref[m], tiles[m][0], 0.0)
            value = value + jnp.where(source_energy == energy + shift_ref[m], tiles[m][1], 0.0)
        rows.append(value)
    kernel = jnp.concatenate(rows, axis=0)
    kernel_hi = kernel.astype(BF16)
    kernel_lo = (kernel - kernel_hi.astype(F32)).astype(BF16)
    for s in range(0, 18, 2):
        value = jnp.concatenate(
            [in_ref[pl.ds(s + k, 128, stride=18), :] for k in range(2)], axis=1
        )
        hi = value.astype(BF16)
        lo = (value - hi.astype(F32)).astype(BF16)
        total = jnp.dot(kernel_hi, hi, preferred_element_type=F32)
        total = total + jnp.dot(kernel_lo, hi, preferred_element_type=F32)
        total = total + jnp.dot(kernel_hi, lo, preferred_element_type=F32)
        for k in range(2):
            out_ref[pl.ds(s + k, 128, stride=18), :] = total[:, 128 * k : 128 * (k + 1)]


def convolve(mode_shift, phonon_kernel, rows):
    return pl.pallas_call(
        convolve_kernel,
        out_shape=jax.ShapeDtypeStruct((ROWS, 128), F32),
        in_specs=[smem(), vmem(), vmem()],
        out_specs=vmem(),
        compiler_params=pltpu.CompilerParams(vmem_limit_bytes=32 * 2**20),
        name="convolve",
    )(mode_shift, phonon_kernel, rows)


def natural_kernel(in_ref, out_ref):
    lane = iota(1)
    orbital_i = (lane // 4) % 4
    part = (lane // 16) % 2
    inner = lane // 32
    orbital_j = lane % 4

    def one(index, carry):
        cell = index // BLOCKS
        block = index % BLOCKS
        source = [
            [in_ref[pl.ds(pair_row(cell, block, i, u), 8), :] for u in range(3)] for i in range(4)
        ]
        for g in range(12):
            if g < 8:
                lane_index = 16 * g + 4 * inner + orbital_j
                options = [(i, t, source[i][t]) for i in range(4) for t in range(2)]
                chosen = 2 * orbital_i + part
            else:
                lane_index = 64 * part + 16 * (g - 8) + 4 * inner + orbital_j
                options = [(i, 0, source[i][2]) for i in range(4)]
                chosen = 2 * orbital_i
            value = lanes(options[0][2], lane_index)
            for i, t, option in options[1:]:
                value = jnp.where(chosen == 2 * i + t, lanes(option, lane_index), value)
            out_ref[pl.ds(block * 8 * 24 + g * 2 + cell, 8, stride=24), :] = value
        return carry

    lax.fori_loop(0, 2 * BLOCKS, one, 0)


def natural(rows):
    return pl.pallas_call(
        natural_kernel,
        out_shape=jax.ShapeDtypeStruct((ROWS, 128), F32),
        in_specs=[vmem()],
        out_specs=vmem(),
        compiler_params=pltpu.CompilerParams(vmem_limit_bytes=32 * 2**20),
        name="natural",
    )(rows)


def rows_of(sigma):
    return sigma.reshape(2, PAIR_COLS // 128, 128).transpose(1, 0, 2).reshape(ROWS, 128)


def exchange(rows):
    parts = rows.reshape(128, 9, 2, 128)
    moved = lax.all_to_all(parts, ("energy", "momentum"), split_axis=0, concat_axis=0, tiled=True)
    return moved.reshape(ROWS, 128)


def body(hopping, coupling, onsite, sigma_in, neighbor_shift, mode_shift, phonon_kernel):
    energies = lax.axis_size("energy")
    energy = 2.0 * (lax.axis_index("energy").astype(F32) + 0.5) / energies
    pairs = green_pairs(
        energy.reshape(1),
        neighbor_shift,
        onsite,
        rows_of(sigma_in),
        hopping.reshape(4, ORB, ORB),
        coupling.reshape(2, ORB, ORB),
    )
    convolved = convolve(mode_shift, phonon_kernel, exchange(pairs))
    result = natural(exchange(convolved))
    result = result.reshape(PAIR_COLS // 128, 2, 128).transpose(1, 0, 2)
    return result.reshape(1, 1, 2, PAIR_COLS)


def solution(mesh):
    return jax.shard_map(
        body,
        mesh=mesh,
        in_specs=(
            P("momentum", None, None, None, None),
            P("momentum", None, None, None),
            P(),
            P("energy", "momentum", None, None),
            P(),
            P(),
            P(),
        ),
        out_specs=P("energy", "momentum", None, None),
        check_vma=False,
    )
```

time: 2120 us -> 115 us (0.05); the launches traced: 2080 us -> 115 us
  other arithmetic: 1080 us -> 0 us
  local copies, waits for them, and re-layouts: 895 us -> 1.45 us
  Pallas kernels: 0 us -> 56.8 us
  matrix products: 53.3 us -> 0 us
  blocking collectives: 24.6 us -> 56.4 us
    unnamed x5 -> x0, other arithmetic: 1020 us -> none
    another operation x14 -> x0, local copies, waits for them, and re-layouts: 280 us -> none  [the longest x8 180 us: pick_pairs(): jnp.stack([matrix_pair[0], matrix_pair[1]])]
    gather x8 -> x0, local copies, waits for them, and re-layouts: 180 us -> none  [the longest x2 166 us: pick_pairs(): return stacked[:, row_atom, :, col_atom, :].reshape(PAIR_COLS)]
    squeeze x8 -> x0, local copies, waits for them, and re-layouts: 136 us -> none  [the longest x4 70.6 us: place_pairs(): return (placed[0], placed[1])]
    sub x10 -> x0, local copies, waits for them, and re-layouts: 109 us -> none  [the longest x2 27.8 us: green_point(): jnp.diag(energy_real - onsite[cell_index]) - hopping_block[cell_index, 0]]
    unnamed x87 -> x5, local copies, waits for them, and re-layouts: 78.4 us -> 1.45 us
    pallas_call x0 -> x3, Pallas kernels: none -> 56.8 us  [the longest x1 49.3 us: green_pairs(): pl.pallas_call(green_kernel, out_shape=jax.ShapeDtypeStruct((ROWS, 128),...]
    add x5 -> x0, local copies, waits for them, and re-layouts: 55.1 us -> none  [the longest x2 27.6 us: complex_product(): second_pair[0] + second_pair[1]]
  transfers between devices with their start and end apart: 1 -> 0, of which waited for: 1 -> 0; matrix products, arithmetic and copies ran while one was open for 0% -> 0% of each run, Pallas kernels for 0% -> 0%
where the time goes in v1:
time: 115 us
  Pallas kernels  56.8 us (49%)
  blocking collectives  56.4 us (49%)
  local copies, waits for them, and re-layouts  1.45 us (1%)
    all_to_all x2, blocking collectives, exchange(): lax.all_to_all(parts, ('energy', 'momentum'), split_axis=0, concat_axis=0...  56.4 us
    pallas_call x1, Pallas kernels, green_pairs(): pl.pallas_call(green_kernel, out_shape=jax.ShapeDtypeStruct((ROWS, 128),...  49.3 us
    pallas_call x1, Pallas kernels, natural(): pl.pallas_call(natural_kernel, out_shape=jax.ShapeDtypeStruct((ROWS, 128)...  6.07 us

profile of v1, /device:TPU:1, one launch (start us, length us, event | category | flops | bytes accessed | tf_op | source)
XLA Modules:
  0.0 114.6 jit_solution(4714301127720058364)
XLA Ops:
  0.0 1.4 %copy.9.shift_in_ref = s32[96,48]{1,0:T(8,128)} copy(s32[96,48]{0,1:T(8,128)} %param.11) | data formatting | bytes 36864 | tf_op args[4]
  1.4 49.3 %green_pairs.1 = f32[2304,128]{1,0:T(8,128)} custom-call(f32[1]{0:T(128)} %bitcast.energy_ref, s32[96,48]{1,0:T(8,128)} %copy.9.shift_in_ref, f32[2,384]{1,0:T(2,128)} %onsite_ref.1, f32[2304,128]{1,0:T(8,128)} %bitcast.22, f32[4,384,384]{2,1,0:T(8,128)} %bitcast.21, f32[2,384,384]{2,1,0:T(8,128)} %bitcast.23), custom_call_target="tpu_custom_call" | custom-call | tf_op jit(solution)/shard_map/green_pairs/pallas_call | solution.py:381
  50.8 0.0 copy-start
  50.8 0.0 copy-start.1
  50.8 31.8 %all_to_all.10 = f32[128,9,2,128]{3,2,1,0:T(2,128)S(1)} all-to-all(f32[128,9,2,128]{3,2,1,0:T(2,128)} %bitcast.20), channel_id=1, replica_groups=mesh['energy'=16,'momentum'=8] {'energy','momentum'}, dimensions={0} | all-to-all | bytes 2359296 | tf_op jit(solution)/shard_map/all_to_all | solution.py:502
  82.6 0.0 copy-done
  82.6 0.0 copy-done.1
  82.6 1.4 %convolve.1 = f32[2304,128]{1,0:T(8,128)S(1)} custom-call(s32[6]{0:T(128)S(1)} %copy-done.1, f32[6,2,8,8]{3,2,1,0:T(8,128)S(1)} %copy-done, f32[2304,128]{1,0:T(8,128)S(1)} %bitcast.18), custom_call_target="tpu_custom_call" | custom-call | tf_op jit(solution)/shard_map/convolve/pallas_call | solution.py:444
  84.0 24.6 %all_to_all.11 = f32[128,9,2,128]{3,2,1,0:T(2,128)S(1)} all-to-all(f32[128,9,2,128]{3,2,1,0:T(2,128)S(1)} %bitcast.19), channel_id=1, replica_groups=mesh['energy'=16,'momentum'=8] {'energy','momentum'}, dimensions={0} | all-to-all | bytes 2359296 | tf_op jit(solution)/shard_map/all_to_all | solution.py:502
  108.6 6.1 %natural.1 = f32[2304,128]{1,0:T(8,128)} custom-call(f32[2304,128]{1,0:T(8,128)S(1)} %bitcast.17), custom_call_target="tpu_custom_call" | custom-call | tf_op jit(solution)/shard_map/natural/pallas_call | solution.py:486
Async XLA Ops:
  50.8 31.8 %copy-start = (f32[6,2,8,8]{3,2,1,0:T(8,128)S(1)}, f32[6,2,8,8]{3,2,1,0:T(8,128)}, u32[]{:S(2)}) copy-start(f32[6,2,8,8]{3,2,1,0:T(8,128)} %phonon_ref.1) | copy-start | bytes 9220
  50.8 31.8 %copy-start.1 = (s32[6]{0:T(128)S(1)}, s32[6]{0:T(128)}, u32[]{:S(2)}) copy-start(s32[6]{0:T(128)} %shift_ref.1) | copy-start | bytes 76

commit v2 on v1

v2 whole, which is shorter than its diff:
```python
import jax
import jax.numpy as jnp
from jax import lax
from jax.experimental import pallas as pl
from jax.experimental.pallas import tpu as pltpu
from jax.sharding import PartitionSpec as P

ORB = 384
ATOMS = 96
NEIGH = 48
PAIR_COLS = 147456
MODES = 6
BROADENING = 0.5
BLOCKS = ATOMS // 8
ROWS = 2 * PAIR_COLS // 128
STRIP = 32
DUO = 2 * ORB
TILES = DUO // 128
GROUPS = ATOMS // 4

F32 = jnp.float32
BF16 = jnp.bfloat16


def lanes(table, index):
    return jnp.take_along_axis(table, index, axis=1, mode="promise_in_bounds")


def iota(dim):
    return lax.broadcasted_iota(jnp.int32, (8, 128), dim)


def pair_row(cell, block, orbital, part):
    return pl.multiple_of((((cell * BLOCKS + block) * 4 + orbital) * 3 + part) * 8, 8)


def split(value):
    hi = value.astype(BF16)
    return hi, (value - hi.astype(F32)).astype(BF16)


def to_left(left, tile, parts, rows=slice(None)):
    for ref, part in zip(left, parts):
        ref[rows, 128 * tile : 128 * (tile + 1)] = part


def to_right(right, tile, parts, row=0, count=ORB):
    upper, lower = pl.ds(row, count), pl.ds(row + ORB, count)
    same = slice(128 * tile, 128 * (tile + 1))
    other = (tile + 3) % TILES
    across = slice(128 * other, 128 * (other + 1))
    for ref, part in zip(right, parts):
        ref[upper, same] = part
        ref[lower, across] = part if tile < 3 else -part


def product(left, right, emit, side=None):
    for step in range(3):
        cols = slice(256 * step, 256 * (step + 1))
        total = jnp.dot(left[0][...], right[0][:, cols], preferred_element_type=F32)
        total = total + jnp.dot(left[1][...], right[0][:, cols], preferred_element_type=F32)
        total = total + jnp.dot(left[0][...], right[1][:, cols], preferred_element_type=F32)
        if side is not None:
            side(step)
        for half in range(2):
            emit(2 * step + half, total[:, 128 * half : 128 * (half + 1)])


def fill_tables(shift_ref, table_ref):
    wide = jnp.concatenate([shift_ref[...], jnp.zeros((NEIGH, 128 - ATOMS), jnp.int32)], axis=1)
    wide = jnp.concatenate([wide, jnp.zeros((128 - NEIGH, 128), jnp.int32)], axis=0)
    shift = wide.T
    lane = iota(1)
    for block in range(BLOCKS):
        col = shift[8 * block : 8 * (block + 1), :] + iota(0) + 8 * block
        col = jnp.where(col >= ATOMS, col - ATOMS, col)
        table_ref[0, 8 * block : 8 * (block + 1), :] = lanes(col, lane // 4)
        table_ref[1, 8 * block : 8 * (block + 1), :] = lanes(col, 32 + (lane % 64) // 4)


def place_group(shift_ref, sigma_ref, spread_ref, placed, group):
    start = pl.multiple_of(group * 96, 32)
    values = jnp.concatenate([sigma_ref[pl.ds(start, 96), :], jnp.zeros((32, 128), F32)], axis=0).T
    lane = lax.broadcasted_iota(jnp.int32, (NEIGH, 128), 1)
    n = lax.broadcasted_iota(jnp.int32, (NEIGH, 128), 0)
    atom = lax.rem(lane // 24, 4) + 4 * group
    wide = jnp.concatenate([shift_ref[...], jnp.zeros((NEIGH, 128 - ATOMS), jnp.int32)], axis=1)
    shift = jnp.concatenate([lanes(wide[8 * k : 8 * (k + 1)], atom[:8]) for k in range(NEIGH // 8)], axis=0)
    col = shift + atom
    col = jnp.where(col >= ATOMS, col - ATOMS, col).astype(F32)
    column = lax.broadcasted_iota(jnp.int32, (128, 128), 0).astype(F32)
    hot = []
    for inner in range(4):
        chosen = jnp.sum(jnp.where(n == 4 * ((lane % 24) // 2) + inner, col, 0.0), axis=0, keepdims=True)
        chosen = jnp.where(lane[0:1] < 96, chosen, -1.0)
        hot.append(jnp.where(column == chosen, 1.0, 0.0).astype(BF16))
    hot = jnp.concatenate(hot, axis=1)
    lane16 = lax.broadcasted_iota(jnp.int32, (16, 128), 1)
    kept = [
        [jnp.where((lane16 // 24 == a) & (lane16 % 2 == cell), 1.0, 0.0).astype(BF16) for a in range(4)]
        for cell in range(2)
    ]
    rows = []
    for part in split(values):
        for cell in range(2):
            for t in range(2):
                for a in range(4):
                    rows.append(
                        jnp.concatenate(
                            [part[32 * k + 16 * t : 32 * k + 16 * (t + 1)] * kept[cell][a] for k in range(4)], axis=1
                        )
                    )
    spread = lax.dot_general(
        jnp.concatenate(rows, axis=0), hot, (((1,), (1,)), ((), ())), preferred_element_type=F32
    )
    spread_ref[...] = spread[0:256] + spread[256:512]
    for j in range(4):
        parts = split(spread_ref[pl.ds(j, 64, stride=4), :])
        for ref, part in zip(placed, parts):
            for ct in range(4):
                ref[pl.ds(pl.multiple_of(ORB * ct + 16 * group, 16), 16), 128 * j : 128 * (j + 1)] = part[
                    16 * ct : 16 * (ct + 1)
                ]


def assemble(placed, hop_ref, systems):
    at = lax.broadcasted_iota(jnp.int32, (512, ORB), 0)
    to = lax.broadcasted_iota(jnp.int32, (512, ORB), 1)
    order = jnp.where((at % 128 < ATOMS) & (to == 4 * (at % 128) + at // 128), 1.0, 0.0).astype(BF16)
    for cell in range(2):
        for t in range(2):
            rows = slice(ORB * (2 * cell + t), ORB * (2 * cell + t + 1))
            value = jnp.dot(placed[0][rows, :], order, preferred_element_type=F32)
            value = value + jnp.dot(placed[1][rows, :], order, preferred_element_type=F32)
            value = -hop_ref[2 * cell + t] - value
            for v in range(3):
                systems[cell][3 * t + v] = value[:, 128 * v : 128 * (v + 1)]


def pick_block(green, table_ref, out_ref, cell, block):
    lane = iota(1)
    orbital_j = lane % 4
    rows8 = pl.ds(pl.multiple_of(8 * block, 8), 8)
    source = [
        [green[s, pl.ds(32 * block + i, 8, stride=4), :] for s in range(TILES)] for i in range(4)
    ]
    for late in range(2):
        col = table_ref[late, rows8, :]
        index = (4 * col + orbital_j) % 128
        chosen = col // 32
        moved = [[lanes(value, index) for value in source[i]] for i in range(4)]
        for i in range(4):
            picked = []
            for t in range(2):
                first, second, third = moved[i][3 * t : 3 * t + 3]
                picked.append(jnp.where(chosen == 0, first, jnp.where(chosen == 1, second, third)))
            if late:
                value = jnp.where(lane < 64, picked[0], picked[1])
                out_ref[pl.ds(pair_row(cell, block, i, 2), 8), :] = value
            else:
                for t in range(2):
                    out_ref[pl.ds(pair_row(cell, block, i, t), 8), :] = picked[t]


def inverse_diagonal(shift, onsite_ref, cell, system, row_ref, col_ref):
    eye = lax.broadcasted_iota(jnp.int32, (128, 128), 0) == lax.broadcasted_iota(jnp.int32, (128, 128), 1)
    for v in range(3):
        cols = slice(128 * v, 128 * (v + 1))
        real = system[v, cols, :] + (shift - onsite_ref[cell : cell + 1, cols])
        imag = system[3 + v, cols, :] + BROADENING
        real, imag = jnp.where(eye, real, 0.0), jnp.where(eye, imag, 0.0)
        for axis, ref in ((0, row_ref), (1, col_ref)):
            down_real = jnp.sum(real, axis=axis, keepdims=True)
            down_imag = jnp.sum(imag, axis=axis, keepdims=True)
            scale = 1.0 / (down_real * down_real + down_imag * down_imag)
            for t, part in enumerate((down_real * scale, -down_imag * scale)):
                if axis == 0:
                    ref[t : t + 1, cols] = part
                else:
                    ref[t, cols, :] = jnp.broadcast_to(part, (128, 128))


def scale_strip(system, row_ref, col_ref, base, left, right, row):
    rows = pl.ds(row, STRIP)
    down_real, down_imag = col_ref[0, rows, :], col_ref[1, rows, :]
    at = lax.broadcasted_iota(jnp.int32, (STRIP, 128), 0) + row
    for v in range(3):
        on = at == lax.broadcasted_iota(jnp.int32, (STRIP, 128), 1) + 128 * v
        across_real = row_ref[0:1, 128 * v : 128 * (v + 1)]
        across_imag = row_ref[1:2, 128 * v : 128 * (v + 1)]
        real = jnp.where(on, 0.0, system[v, rows, :])
        imag = jnp.where(on, 0.0, system[3 + v, rows, :])
        real, imag = real * across_real - imag * across_imag, real * across_imag + imag * across_real
        to_right(right, v, split(real), row, STRIP)
        to_right(right, 3 + v, split(imag), row, STRIP)
        real, imag = down_real * real - down_imag * imag, down_real * imag + down_imag * real
        to_left(left, v, split(real), rows)
        to_left(left, 3 + v, split(imag), rows)
        base[v, rows, :] = jnp.where(on, down_real, 0.0) - real
        base[3 + v, rows, :] = jnp.where(on, down_imag, 0.0) - imag


def strips(step, unroll=2):
    def one(index, carry):
        step(pl.multiple_of(index * STRIP, STRIP))
        return carry

    lax.fori_loop(0, ORB // STRIP, one, 0, unroll=unroll)


def green_kernel(
    energy_ref,
    shift_ref,
    onsite_ref,
    sigma_ref,
    hop_in_ref,
    coup_in_ref,
    out_ref,
    table_ref,
    spread_ref,
    row_ref,
    col_ref,
    hop_ref,
    coup_ref,
    first_system,
    second_system,
    base,
    green,
    placed_hi,
    placed_lo,
    sems,
    *operands,
):
    duos = [(operands[2 * s], operands[2 * s + 1]) for s in range(len(operands) // 2)]
    left_a, left_b, left_v, left_u, right_a, right_b, right_v = duos
    hop_copy = pltpu.make_async_copy(hop_in_ref, hop_ref, sems.at[0])
    coup_copy = pltpu.make_async_copy(coup_in_ref, coup_ref, sems.at[1])
    hop_copy.start()
    coup_copy.start()
    energy = energy_ref[0]
    placed = (placed_hi, placed_lo)
    fill_tables(shift_ref, table_ref)

    def place(group, carry):
        place_group(shift_ref, sigma_ref, spread_ref, placed, group)
        return carry

    lax.fori_loop(0, GROUPS, place, 0, unroll=2)
    hop_copy.wait()
    assemble(placed, hop_ref, (first_system, second_system))
    coup_copy.wait()
    for t in range(2):
        turned = coup_ref[t].T
        for v in range(3):
            cols = slice(128 * v, 128 * (v + 1))
            to_right(right_v, 3 * t + v, split(coup_ref[t, :, cols]))
            to_left(left_v, 3 * t + v, split(turned[:, cols] if t == 0 else -turned[:, cols]))

    def second_term(tile, value):
        to_left(left_b, tile, split(value))
        base[tile] += value

    def invert(cell, system, emit):
        inverse_diagonal(energy, onsite_ref, cell, system, row_ref, col_ref)
        strips(lambda row: scale_strip(system, row_ref, col_ref, base, left_a, right_a, row))
        product(left_a, right_a, second_term)
        product(left_b, right_a, lambda tile, value: emit(tile, base[tile] - value))

    def first_green(tile, value):
        green[tile] = value
        parts = split(value)
        to_left(left_a, tile, parts)
        to_right(right_b, tile, parts)

    invert(0, first_system, first_green)

    def adjoint(tile, value):
        parts = split(value)
        to_left(left_b, tile, parts)
        to_right(right_a, tile, parts)

    product(left_v, right_b, adjoint)

    def fold(tile, value):
        second_system[tile] -= value

    product(left_b, right_v, fold)
    product(left_a, right_v, lambda tile, value: to_left(left_u, tile, split(value)))
    inverse_diagonal(energy, onsite_ref, 1, second_system, row_ref, col_ref)
    strips(lambda row: scale_strip(second_system, row_ref, col_ref, base, left_a, right_b, row))
    product(left_a, right_b, second_term)

    def second_green(tile, value):
        value = base[tile] - value
        first_system[tile] = value
        to_right(right_v, tile, split(value))

    product(left_b, right_b, second_green)

    def pick_second(step):
        for block in range(4 * step, 4 * step + 4):
            pick_block(first_system, table_ref, out_ref, 1, block)

    product(left_u, right_v, lambda tile, value: to_left(left_b, tile, split(value)), pick_second)

    def through(tile, value):
        green[tile] += value

    product(left_b, right_a, through)

    def pick(block, carry):
        pick_block(green, table_ref, out_ref, 0, block)
        return carry

    lax.fori_loop(0, BLOCKS, pick, 0, unroll=3)


def vmem():
    return pl.BlockSpec(memory_space=pltpu.VMEM)


def smem():
    return pl.BlockSpec(memory_space=pltpu.SMEM)


def green_pairs(energy, neighbor_shift, onsite, sigma_rows, hopping, coupling):
    left = [pltpu.VMEM((ORB, DUO), BF16)] * 2
    right = [pltpu.VMEM((DUO, DUO), BF16)] * 2
    return pl.pallas_call(
        green_kernel,
        out_shape=jax.ShapeDtypeStruct((ROWS, 128), F32),
        in_specs=[smem()] + [vmem()] * 3 + [pl.BlockSpec(memory_space=pl.ANY)] * 2,
        out_specs=vmem(),
        scratch_shapes=[
            pltpu.VMEM((2, ATOMS, 128), jnp.int32),
            pltpu.VMEM((256, 128), F32),
            pltpu.VMEM((8, ORB), F32),
            pltpu.VMEM((2, ORB, 128), F32),
            pltpu.VMEM((4, ORB, ORB), F32),
            pltpu.VMEM((2, ORB, ORB), F32),
            pltpu.VMEM((TILES, ORB, 128), F32),
            pltpu.VMEM((TILES, ORB, 128), F32),
            pltpu.VMEM((TILES, ORB, 128), F32),
            pltpu.VMEM((TILES, ORB, 128), F32),
            pltpu.VMEM((4 * ORB, 512), BF16),
            pltpu.VMEM((4 * ORB, 512), BF16),
            pltpu.SemaphoreType.DMA((2,)),
            *left,
            *left,
            *left,
            *left,
            *right,
            *right,
            *right,
        ],
        compiler_params=pltpu.CompilerParams(vmem_limit_bytes=56 * 2**20),
        name="green_pairs",
    )(energy, neighbor_shift.T, onsite, sigma_rows, hopping, coupling)


def convolve_kernel(shift_ref, phonon_ref, in_ref, out_ref):
    source_energy = iota(1) // 8
    momentum = iota(1) % 8
    tiles = []
    for m in range(MODES):
        pair = []
        for d in range(2):
            wide = jnp.concatenate([phonon_ref[m, d]] * 16, axis=1)
            pair.append(wide)
        tiles.append(pair)
    rows = []
    for energy in range(16):
        value = jnp.zeros((8, 128), F32)
        for m in range(MODES):
            value = value + jnp.where(source_energy == energy - shift_ref[m], tiles[m][0], 0.0)
            value = value + jnp.where(source_energy == energy + shift_ref[m], tiles[m][1], 0.0)
        rows.append(value)
    kernel = jnp.concatenate(rows, axis=0)
    kernel_hi = kernel.astype(BF16)
    kernel_lo = (kernel - kernel_hi.astype(F32)).astype(BF16)
    for s in range(0, 18, 2):
        value = jnp.concatenate(
            [in_ref[pl.ds(s + k, 128, stride=18), :] for k in range(2)], axis=1
        )
        hi = value.astype(BF16)
        lo = (value - hi.astype(F32)).astype(BF16)
        total = jnp.dot(kernel_hi, hi, preferred_element_type=F32)
        total = total + jnp.dot(kernel_lo, hi, preferred_element_type=F32)
        total = total + jnp.dot(kernel_hi, lo, preferred_element_type=F32)
        for k in range(2):
            out_ref[pl.ds(s + k, 128, stride=18), :] = total[:, 128 * k : 128 * (k + 1)]


def convolve(mode_shift, phonon_kernel, rows):
    return pl.pallas_call(
        convolve_kernel,
        out_shape=jax.ShapeDtypeStruct((ROWS, 128), F32),
        in_specs=[smem(), vmem(), vmem()],
        out_specs=vmem(),
        compiler_params=pltpu.CompilerParams(vmem_limit_bytes=32 * 2**20),
        name="convolve",
    )(mode_shift, phonon_kernel, rows)


def natural_kernel(in_ref, out_ref):
    lane = iota(1)
    orbital_i = (lane // 4) % 4
    part = (lane // 16) % 2
    inner = lane // 32
    orbital_j = lane % 4

    def one(index, carry):
        cell = index // BLOCKS
        block = index % BLOCKS
        source = [
            [in_ref[pl.ds(pair_row(cell, block, i, u), 8), :] for u in range(3)] for i in range(4)
        ]
        for g in range(12):
            if g < 8:
                lane_index = 16 * g + 4 * inner + orbital_j
                options = [(i, t, source[i][t]) for i in range(4) for t in range(2)]
                chosen = 2 * orbital_i + part
            else:
                lane_index = 64 * part + 16 * (g - 8) + 4 * inner + orbital_j
                options = [(i, 0, source[i][2]) for i in range(4)]
                chosen = 2 * orbital_i
            value = lanes(options[0][2], lane_index)
            for i, t, option in options[1:]:
                value = jnp.where(chosen == 2 * i + t, lanes(option, lane_index), value)
            out_ref[pl.ds(block * 8 * 24 + g * 2 + cell, 8, stride=24), :] = value
        return carry

    lax.fori_loop(0, 2 * BLOCKS, one, 0, unroll=3)


def natural(rows):
    return pl.pallas_call(
        natural_kernel,
        out_shape=jax.ShapeDtypeStruct((ROWS, 128), F32),
        in_specs=[vmem()],
        out_specs=vmem(),
        compiler_params=pltpu.CompilerParams(vmem_limit_bytes=32 * 2**20),
        name="natural",
    )(rows)


def rows_of(sigma):
    return sigma.reshape(2, PAIR_COLS // 128, 128).transpose(1, 0, 2).reshape(ROWS, 128)


def exchange(rows):
    parts = rows.reshape(128, 9, 2, 128)
    moved = lax.all_to_all(parts, ("energy", "momentum"), split_axis=0, concat_axis=0, tiled=True)
    return moved.reshape(ROWS, 128)


def body(hopping, coupling, onsite, sigma_in, neighbor_shift, mode_shift, phonon_kernel):
    energies = lax.axis_size("energy")
    energy = 2.0 * (lax.axis_index("energy").astype(F32) + 0.5) / energies
    pairs = green_pairs(
        energy.reshape(1),
        neighbor_shift,
        onsite,
        rows_of(sigma_in),
        hopping.reshape(4, ORB, ORB),
        coupling.reshape(2, ORB, ORB),
    )
    convolved = convolve(mode_shift, phonon_kernel, exchange(pairs))
    result = natural(exchange(convolved))
    result = result.reshape(PAIR_COLS // 128, 2, 128).transpose(1, 0, 2)
    return result.reshape(1, 1, 2, PAIR_COLS)


def solution(mesh):
    return jax.shard_map(
        body,
        mesh=mesh,
        in_specs=(
            P("momentum", None, None, None, None),
            P("momentum", None, None, None),
            P(),
            P("energy", "momentum", None, None),
            P(),
            P(),
            P(),
        ),
        out_specs=P("energy", "momentum", None, None),
        check_vma=False,
    )
```

time: 115 us -> 94.7 us (0.82)
  Pallas kernels: 56.8 us -> 38.1 us
  local copies, waits for them, and re-layouts: 1.45 us -> 0.01 us
    pallas_call x1, Pallas kernels: 49.3 us -> 32 us  [green_pairs(): pl.pallas_call(green_kernel, out_shape=jax.ShapeDtypeStruct((ROWS, 128),...]
    unnamed x5 -> x4, local copies, waits for them, and re-layouts: 1.45 us -> 0.01 us
    pallas_call x1, Pallas kernels: 6.07 us -> 4.66 us  [natural(): pl.pallas_call(natural_kernel, out_shape=jax.ShapeDtypeStruct((ROWS, 128)...]
where the time goes in v2:
time: 94.7 us; the launch traced here: 94.5 us
  blocking collectives  56.4 us (60%)
  Pallas kernels  38.1 us (40%)
    all_to_all x2, blocking collectives, exchange(): lax.all_to_all(parts, ('energy', 'momentum'), split_axis=0, concat_axis=0...  56.4 us
    pallas_call x1, Pallas kernels, green_pairs(): pl.pallas_call(green_kernel, out_shape=jax.ShapeDtypeStruct((ROWS, 128),...  32 us
    pallas_call x1, Pallas kernels, natural(): pl.pallas_call(natural_kernel, out_shape=jax.ShapeDtypeStruct((ROWS, 128)...  4.66 us

profile of v2, /device:TPU:1, one launch (start us, length us, event | category | flops | bytes accessed | tf_op | source)
XLA Modules:
  0.0 94.5 jit_solution(8015157261417884849)
XLA Ops:
  0.0 32.0 %green_pairs.1 = f32[2304,128]{1,0:T(8,128)} custom-call(f32[1]{0:T(128)} %bitcast.energy_ref, s32[48,96]{1,0:T(8,128)} %bitcast.25, f32[2,384]{1,0:T(2,128)} %onsite_ref.1, f32[2304,128]{1,0:T(8,128)} %bitcast.23, f32[4,384,384]{2,1,0:T(8,128)} %bitcast.22, f32[2,384,384]{2,1,0:T(8,128)} %bitcast.24), custom_call_target="tpu_custom_call" | custom-call | tf_op jit(solution)/shard_map/green_pairs/pallas_call | solution.py:329
  32.0 0.0 copy-start
  32.0 0.0 copy-start.1
  32.0 31.8 %all_to_all.10 = f32[128,9,2,128]{3,2,1,0:T(2,128)S(1)} all-to-all(f32[128,9,2,128]{3,2,1,0:T(2,128)} %bitcast.21), channel_id=1, replica_groups=mesh['energy'=16,'momentum'=8] {'energy','momentum'}, dimensions={0} | all-to-all | bytes 2359296 | tf_op jit(solution)/shard_map/all_to_all | solution.py:453
  63.8 0.0 copy-done
  63.8 0.0 copy-done.1
  63.8 1.4 %convolve.1 = f32[2304,128]{1,0:T(8,128)S(1)} custom-call(s32[6]{0:T(128)S(1)} %copy-done.1, f32[6,2,8,8]{3,2,1,0:T(8,128)S(1)} %copy-done, f32[2304,128]{1,0:T(8,128)S(1)} %bitcast.19), custom_call_target="tpu_custom_call" | custom-call | tf_op jit(solution)/shard_map/convolve/pallas_call | solution.py:395
  65.3 24.6 %all_to_all.11 = f32[128,9,2,128]{3,2,1,0:T(2,128)S(1)} all-to-all(f32[128,9,2,128]{3,2,1,0:T(2,128)S(1)} %bitcast.20), channel_id=1, replica_groups=mesh['energy'=16,'momentum'=8] {'energy','momentum'}, dimensions={0} | all-to-all | bytes 2359296 | tf_op jit(solution)/shard_map/all_to_all | solution.py:453
  89.8 4.7 %natural.1 = f32[2304,128]{1,0:T(8,128)} custom-call(f32[2304,128]{1,0:T(8,128)S(1)} %bitcast.18), custom_call_target="tpu_custom_call" | custom-call | tf_op jit(solution)/shard_map/natural/pallas_call | solution.py:437
Async XLA Ops:
  32.0 31.8 %copy-start = (f32[6,2,8,8]{3,2,1,0:T(8,128)S(1)}, f32[6,2,8,8]{3,2,1,0:T(8,128)}, u32[]{:S(2)}) copy-start(f32[6,2,8,8]{3,2,1,0:T(8,128)} %phonon_ref.1) | copy-start | bytes 9220
  32.0 31.8 %copy-start.1 = (s32[6]{0:T(128)S(1)}, s32[6]{0:T(128)}, u32[]{:S(2)}) copy-start(s32[6]{0:T(128)} %shift_ref.1) | copy-start | bytes 76

commit v3 on v2

--- a/solution.py
+++ b/solution.py
@@ -30,10 +30,6 @@
     return lax.broadcasted_iota(jnp.int32, (8, 128), dim)
 
 
-def pair_row(cell, block, orbital, part):
-    return pl.multiple_of((((cell * BLOCKS + block) * 4 + orbital) * 3 + part) * 8, 8)
-
-
 def split(value):
     hi = value.astype(BF16)
     return hi, (value - hi.astype(F32)).astype(BF16)
@@ -54,12 +50,12 @@
         ref[lower, across] = part if tile < 3 else -part
 
 
-def product(left, right, emit, side=None):
+def product(left, right, emit, side=None, rows=slice(None)):
     for step in range(3):
         cols = slice(256 * step, 256 * (step + 1))
-        total = jnp.dot(left[0][...], right[0][:, cols], preferred_element_type=F32)
-        total = total + jnp.dot(left[1][...], right[0][:, cols], preferred_element_type=F32)
-        total = total + jnp.dot(left[0][...], right[1][:, cols], preferred_element_type=F32)
+        total = jnp.dot(left[0][rows, :], right[0][:, cols], preferred_element_type=F32)
+        total = total + jnp.dot(left[1][rows, :], right[0][:, cols], preferred_element_type=F32)
+        total = total + jnp.dot(left[0][rows, :], right[1][:, cols], preferred_element_type=F32)
         if side is not None:
             side(step)
         for half in range(2):
@@ -70,44 +66,64 @@
     wide = jnp.concatenate([shift_ref[...], jnp.zeros((NEIGH, 128 - ATOMS), jnp.int32)], axis=1)
     wide = jnp.concatenate([wide, jnp.zeros((128 - NEIGH, 128), jnp.int32)], axis=0)
     shift = wide.T
-    lane = iota(1)
-    for block in range(BLOCKS):
-        col = shift[8 * block : 8 * (block + 1), :] + iota(0) + 8 * block
-        col = jnp.where(col >= ATOMS, col - ATOMS, col)
-        table_ref[0, 8 * block : 8 * (block + 1), :] = lanes(col, lane // 4)
-        table_ref[1, 8 * block : 8 * (block + 1), :] = lanes(col, 32 + (lane % 64) // 4)
+    for v in range(3):
+        for block in range(BLOCKS):
+            rows = slice(8 * block, 8 * (block + 1))
+            col = shift[rows, :] + iota(0) + 8 * block
+            col = jnp.where(col >= ATOMS, col - ATOMS, col)
+            table_ref[v, rows, :] = lanes(col, 16 * v + iota(1) // 8)
+
+
+def fill_order(order_ref):
+    for start in range(0, 512, 64):
+        at = lax.broadcasted_iota(jnp.int32, (64, 512), 0) + start
+        to = (at % 128) // 8 * 32 + (at // 4) % 2 * 16 + at // 128 * 4 + at % 4
+        hot = to == lax.broadcasted_iota(jnp.int32, (64, 512), 1)
+        order_ref[start : start + 64, :] = jnp.where(hot, 1.0, 0.0).astype(BF16)
 
 
 def place_group(shift_ref, sigma_ref, spread_ref, placed, group):
-    start = pl.multiple_of(group * 96, 32)
-    values = jnp.concatenate([sigma_ref[pl.ds(start, 96), :], jnp.zeros((32, 128), F32)], axis=0).T
+    start = group * 96
+    gap = jnp.zeros((16, 128), F32)
+    cells = [sigma_ref[pl.ds(start + cell, 48, stride=2), :] for cell in range(2)]
+    values = jnp.concatenate([cells[0], gap, cells[1], gap], axis=0).T
+    swapped = pltpu.roll(values, 64, 1)
+    lane32 = lax.broadcasted_iota(jnp.int32, (32, 128), 1)
     lane = lax.broadcasted_iota(jnp.int32, (NEIGH, 128), 1)
     n = lax.broadcasted_iota(jnp.int32, (NEIGH, 128), 0)
-    atom = lax.rem(lane // 24, 4) + 4 * group
+    inner = lane % 64
+    atom = lax.rem(inner // 12, 4) + 4 * group
     wide = jnp.concatenate([shift_ref[...], jnp.zeros((NEIGH, 128 - ATOMS), jnp.int32)], axis=1)
     shift = jnp.concatenate([lanes(wide[8 * k : 8 * (k + 1)], atom[:8]) for k in range(NEIGH // 8)], axis=0)
     col = shift + atom
     col = jnp.where(col >= ATOMS, col - ATOMS, col).astype(F32)
     column = lax.broadcasted_iota(jnp.int32, (128, 128), 0).astype(F32)
     hot = []
-    for inner in range(4):
-        chosen = jnp.sum(jnp.where(n == 4 * ((lane % 24) // 2) + inner, col, 0.0), axis=0, keepdims=True)
-        chosen = jnp.where(lane[0:1] < 96, chosen, -1.0)
+    for duo in range(2):
+        mine = n == 4 * (inner % 12) + 2 * duo + lane // 64
+        chosen = jnp.sum(jnp.where(mine, col, 0.0), axis=0, keepdims=True)
+        chosen = jnp.where(inner[0:1] < 48, chosen, -1.0)
         hot.append(jnp.where(column == chosen, 1.0, 0.0).astype(BF16))
     hot = jnp.concatenate(hot, axis=1)
-    lane16 = lax.broadcasted_iota(jnp.int32, (16, 128), 1)
-    kept = [
-        [jnp.where((lane16 // 24 == a) & (lane16 % 2 == cell), 1.0, 0.0).astype(BF16) for a in range(4)]
-        for cell in range(2)
-    ]
+    inner16 = lax.broadcasted_iota(jnp.int32, (16, 128), 1) % 64
+    kept = [jnp.where(inner16 // 12 == a, 1.0, 0.0).astype(BF16) for a in range(4)]
+    parts = []
+    for cell in range(2):
+        near, far = (values, swapped) if cell == 0 else (swapped, values)
+        parts.append(
+            [
+                split(jnp.where(lane32 < 64, near[64 * duo : 64 * duo + 32], far[64 * duo + 32 : 64 * duo + 64]))
+                for duo in range(2)
+            ]
+        )
     rows = []
-    for part in split(values):
+    for part in range(2):
         for cell in range(2):
             for t in range(2):
                 for a in range(4):
                     rows.append(
                         jnp.concatenate(
-                            [part[32 * k + 16 * t : 32 * k + 16 * (t + 1)] * kept[cell][a] for k in range(4)], axis=1
+                            [parts[cell][duo][part][16 * t : 16 * (t + 1)] * kept[a] for duo in range(2)], axis=1
                         )
                     )
     spread = lax.dot_general(
@@ -115,51 +131,74 @@
     )
     spread_ref[...] = spread[0:256] + spread[256:512]
     for j in range(4):
-        parts = split(spread_ref[pl.ds(j, 64, stride=4), :])
-        for ref, part in zip(placed, parts):
+        pieces = split(spread_ref[pl.ds(j, 64, stride=4), :])
+        for ref, piece in zip(placed, pieces):
             for ct in range(4):
-                ref[pl.ds(pl.multiple_of(ORB * ct + 16 * group, 16), 16), 128 * j : 128 * (j + 1)] = part[
+                ref[pl.ds(pl.multiple_of(ORB * ct + 16 * group, 16), 16), 128 * j : 128 * (j + 1)] = piece[
                     16 * ct : 16 * (ct + 1)
                 ]
 
 
-def assemble(placed, hop_ref, systems):
+def assemble(placed, hop_ref, system, cell, t):
     at = lax.broadcasted_iota(jnp.int32, (512, ORB), 0)
     to = lax.broadcasted_iota(jnp.int32, (512, ORB), 1)
     order = jnp.where((at % 128 < ATOMS) & (to == 4 * (at % 128) + at // 128), 1.0, 0.0).astype(BF16)
-    for cell in range(2):
-        for t in range(2):
-            rows = slice(ORB * (2 * cell + t), ORB * (2 * cell + t + 1))
-            value = jnp.dot(placed[0][rows, :], order, preferred_element_type=F32)
-            value = value + jnp.dot(placed[1][rows, :], order, preferred_element_type=F32)
-            value = -hop_ref[2 * cell + t] - value
-            for v in range(3):
-                systems[cell][3 * t + v] = value[:, 128 * v : 128 * (v + 1)]
-
-
-def pick_block(green, table_ref, out_ref, cell, block):
+    rows = slice(ORB * (2 * cell + t), ORB * (2 * cell + t + 1))
+    value = jnp.dot(placed[0][rows, :], order, preferred_element_type=F32)
+    value = value + jnp.dot(placed[1][rows, :], order, preferred_element_type=F32)
+    value = -hop_ref[2 * cell + t] - value
+    for v in range(3):
+        system[3 * t + v] = value[:, 128 * v : 128 * (v + 1)]
+
+
+def pick_atoms(green, table_ref, picked, start):
     lane = iota(1)
     orbital_j = lane % 4
-    rows8 = pl.ds(pl.multiple_of(8 * block, 8), 8)
+    real = (lane // 4) % 2 == 0
     source = [
-        [green[s, pl.ds(32 * block + i, 8, stride=4), :] for s in range(TILES)] for i in range(4)
+        [
+            [green[s, pl.ds(4 * (start + 8 * half) + i, 8, stride=4), :] for s in range(TILES)]
+            for i in range(4)
+        ]
+        for half in range(2)
     ]
-    for late in range(2):
-        col = table_ref[late, rows8, :]
-        index = (4 * col + orbital_j) % 128
-        chosen = col // 32
-        moved = [[lanes(value, index) for value in source[i]] for i in range(4)]
+    for v in range(3):
+        chosen_values = []
+        for half in range(2):
+            col = table_ref[v, pl.ds(start + 8 * half, 8), :]
+            index = (4 * col + orbital_j) % 128
+            tile = col // 32
+            moved = [[lanes(value, index) for value in source[half][i]] for i in range(4)]
+            chosen_values.append(
+                [
+                    jnp.where(
+                        tile == 0,
+                        jnp.where(real, moved[i][0], moved[i][3]),
+                        jnp.where(
+                            tile == 1,
+                            jnp.where(real, moved[i][1], moved[i][4]),
+                            jnp.where(real, moved[i][2], moved[i][5]),
+                        ),
+                    )
+                    for i in range(4)
+                ]
+            )
+        rows = pl.ds(ATOMS * v + start, 16)
         for i in range(4):
-            picked = []
-            for t in range(2):
-                first, second, third = moved[i][3 * t : 3 * t + 3]
-                picked.append(jnp.where(chosen == 0, first, jnp.where(chosen == 1, second, third)))
-            if late:
-                value = jnp.where(lane < 64, picked[0], picked[1])
-                out_ref[pl.ds(pair_row(cell, block, i, 2), 8), :] = value
-            else:
-                for t in range(2):
-                    out_ref[pl.ds(pair_row(cell, block, i, t), 8), :] = picked[t]
+            value = jnp.concatenate([chosen_values[0][i], chosen_values[1][i]], axis=0)
+            for ref, part in zip(picked, split(value)):
+                ref[rows, 128 * i : 128 * (i + 1)] = part
+
+
+def order_pairs(picked, order_ref, out_ref, cell):
+    value = jnp.dot(picked[0][...], order_ref[...], preferred_element_type=F32)
+    value = value + jnp.dot(picked[1][...], order_ref[...], preferred_element_type=F32)
+    for v in range(3):
+        for block in range(BLOCKS):
+            row = ATOMS * v + 8 * block
+            for g in range(4):
+                to = (block * 8 * 12 + 4 * v + g) * 2 + cell
+                out_ref[pl.ds(to, 8, stride=24), :] = value[row : row + 8, 128 * g : 128 * (g + 1)]
 
 
 def inverse_diagonal(shift, onsite_ref, cell, system, row_ref, col_ref):
@@ -200,14 +239,6 @@
         base[3 + v, rows, :] = jnp.where(on, down_imag, 0.0) - imag
 
 
-def strips(step, unroll=2):
-    def one(index, carry):
-        step(pl.multiple_of(index * STRIP, STRIP))
-        return carry
-
-    lax.fori_loop(0, ORB // STRIP, one, 0, unroll=unroll)
-
-
 def green_kernel(
     energy_ref,
     shift_ref,
@@ -217,6 +248,7 @@
     coup_in_ref,
     out_ref,
     table_ref,
+    order_ref,
     spread_ref,
     row_ref,
     col_ref,
@@ -228,6 +260,10 @@
     green,
     placed_hi,
     placed_lo,
+    picked_hi,
+    picked_lo,
+    more_hi,
+    more_lo,
     sems,
     *operands,
 ):
@@ -239,7 +275,9 @@
     coup_copy.start()
     energy = energy_ref[0]
     placed = (placed_hi, placed_lo)
+    first_picked, second_picked = (picked_hi, picked_lo), (more_hi, more_lo)
     fill_tables(shift_ref, table_ref)
+    fill_order(order_ref)
 
     def place(group, carry):
         place_group(shift_ref, sigma_ref, spread_ref, placed, group)
@@ -247,32 +285,37 @@
 
     lax.fori_loop(0, GROUPS, place, 0, unroll=2)
     hop_copy.wait()
-    assemble(placed, hop_ref, (first_system, second_system))
     coup_copy.wait()
     for t in range(2):
-        turned = coup_ref[t].T
+        assemble(placed, hop_ref, first_system, 0, t)
+    inverse_diagonal(energy, onsite_ref, 0, first_system, row_ref, col_ref)
+    for t in range(2):
+        assemble(placed, hop_ref, second_system, 1, t)
+        for strip in range(6 * t, 6 * t + 6):
+            scale_strip(first_system, row_ref, col_ref, base, left_a, right_a, strip * STRIP)
+
+    def coupling(step):
+        if step == 2:
+            return
+        turned = coup_ref[step].T
         for v in range(3):
             cols = slice(128 * v, 128 * (v + 1))
-            to_right(right_v, 3 * t + v, split(coup_ref[t, :, cols]))
-            to_left(left_v, 3 * t + v, split(turned[:, cols] if t == 0 else -turned[:, cols]))
+            to_right(right_v, 3 * step + v, split(coup_ref[step, :, cols]))
+            to_left(left_v, 3 * step + v, split(turned[:, cols] if step == 0 else -turned[:, cols]))
 
     def second_term(tile, value):
         to_left(left_b, tile, split(value))
         base[tile] += value
 
-    def invert(cell, system, emit):
-        inverse_diagonal(energy, onsite_ref, cell, system, row_ref, col_ref)
-        strips(lambda row: scale_strip(system, row_ref, col_ref, base, left_a, right_a, row))
-        product(left_a, right_a, second_term)
-        product(left_b, right_a, lambda tile, value: emit(tile, base[tile] - value))
-
     def first_green(tile, value):
+        value = base[tile] - value
         green[tile] = value
         parts = split(value)
         to_left(left_a, tile, parts)
         to_right(right_b, tile, parts)
 
-    invert(0, first_system, first_green)
+    product(left_a, right_a, second_term, coupling)
+    product(left_b, right_a, first_green)
 
     def adjoint(tile, value):
         parts = split(value)
@@ -285,10 +328,14 @@
         second_system[tile] -= value
 
     product(left_b, right_v, fold)
-    product(left_a, right_v, lambda tile, value: to_left(left_u, tile, split(value)))
     inverse_diagonal(energy, onsite_ref, 1, second_system, row_ref, col_ref)
-    strips(lambda row: scale_strip(second_system, row_ref, col_ref, base, left_a, right_b, row))
-    product(left_a, right_b, second_term)
+
+    def scale(step):
+        for strip in range(4 * step, 4 * step + 4):
+            scale_strip(second_system, row_ref, col_ref, base, left_v, right_b, strip * STRIP)
+
+    product(left_a, right_v, lambda tile, value: to_left(left_u, tile, split(value)), scale)
+    product(left_v, right_b, second_term)
 
     def second_green(tile, value):
         value = base[tile] - value
@@ -298,21 +345,26 @@
     product(left_b, right_b, second_green)
 
     def pick_second(step):
-        for block in range(4 * step, 4 * step + 4):
-            pick_block(first_system, table_ref, out_ref, 1, block)
-
-    product(left_u, right_v, lambda tile, value: to_left(left_b, tile, split(value)), pick_second)
-
-    def through(tile, value):
-        green[tile] += value
-
-    product(left_b, right_a, through)
-
-    def pick(block, carry):
-        pick_block(green, table_ref, out_ref, 0, block)
-        return carry
-
-    lax.fori_loop(0, BLOCKS, pick, 0, unroll=3)
+        for half in range(2):
+            pick_atoms(first_system, table_ref, second_picked, 32 * step + 16 * half)
+
+    product(left_u, right_v, lambda tile, value: to_left(left_a, tile, split(value)), pick_second)
+    for chunk in range(3):
+        rows = slice(128 * chunk, 128 * (chunk + 1))
+
+        def through(tile, value, rows=rows):
+            green[tile, rows, :] += value
+
+        def beside(step, chunk=chunk):
+            if step == 0 and chunk == 0:
+                order_pairs(second_picked, order_ref, out_ref, 1)
+            if step < 2 and chunk > 0:
+                pick_atoms(green, table_ref, first_picked, 32 * (chunk - 1) + 16 * step)
+
+        product(left_a, right_a, through, beside, rows)
+    for half in range(2):
+        pick_atoms(green, table_ref, first_picked, 64 + 16 * half)
+    order_pairs(first_picked, order_ref, out_ref, 0)
 
 
 def vmem():
@@ -332,7 +384,8 @@
         in_specs=[smem()] + [vmem()] * 3 + [pl.BlockSpec(memory_space=pl.ANY)] * 2,
         out_specs=vmem(),
         scratch_shapes=[
-            pltpu.VMEM((2, ATOMS, 128), jnp.int32),
+            pltpu.VMEM((3, ATOMS, 128), jnp.int32),
+            pltpu.VMEM((512, 512), BF16),
             pltpu.VMEM((256, 128), F32),
             pltpu.VMEM((8, ORB), F32),
             pltpu.VMEM((2, ORB, 128), F32),
@@ -344,6 +397,7 @@
             pltpu.VMEM((TILES, ORB, 128), F32),
             pltpu.VMEM((4 * ORB, 512), BF16),
             pltpu.VMEM((4 * ORB, 512), BF16),
+            *([pltpu.VMEM((3 * ATOMS, 512), BF16)] * 4),
             pltpu.SemaphoreType.DMA((2,)),
             *left,
             *left,
@@ -402,48 +456,6 @@
     )(mode_shift, phonon_kernel, rows)
 
 
-def natural_kernel(in_ref, out_ref):
-    lane = iota(1)
-    orbital_i = (lane // 4) % 4
-    part = (lane // 16) % 2
-    inner = lane // 32
-    orbital_j = lane % 4
-
-    def one(index, carry):
-        cell = index // BLOCKS
-        block = index % BLOCKS
-        source = [
-            [in_ref[pl.ds(pair_row(cell, block, i, u), 8), :] for u in range(3)] for i in range(4)
-        ]
-        for g in range(12):
-            if g < 8:
-                lane_index = 16 * g + 4 * inner + orbital_j
-                options = [(i, t, source[i][t]) for i in range(4) for t in range(2)]
-                chosen = 2 * orbital_i + part
-            else:
-                lane_index = 64 * part + 16 * (g - 8) + 4 * inner + orbital_j
-                options = [(i, 0, source[i][2]) for i in range(4)]
-                chosen = 2 * orbital_i
-            value = lanes(options[0][2], lane_index)
-            for i, t, option in options[1:]:
-                value = jnp.where(chosen == 2 * i + t, lanes(option, lane_index), value)
-            out_ref[pl.ds(block * 8 * 24 + g * 2 + cell, 8, stride=24), :] = value
-        return carry
-
-    lax.fori_loop(0, 2 * BLOCKS, one, 0, unroll=3)
-
-
-def natural(rows):
-    return pl.pallas_call(
-        natural_kernel,
-        out_shape=jax.ShapeDtypeStruct((ROWS, 128), F32),
-        in_specs=[vmem()],
-        out_specs=vmem(),
-        compiler_params=pltpu.CompilerParams(vmem_limit_bytes=32 * 2**20),
-        name="natural",
-    )(rows)
-
-
 def rows_of(sigma):
     return sigma.reshape(2, PAIR_COLS // 128, 128).transpose(1, 0, 2).reshape(ROWS, 128)
 
@@ -466,8 +478,7 @@
         coupling.reshape(2, ORB, ORB),
     )
     convolved = convolve(mode_shift, phonon_kernel, exchange(pairs))
-    result = natural(exchange(convolved))
-    result = result.reshape(PAIR_COLS // 128, 2, 128).transpose(1, 0, 2)
+    result = exchange(convolved).reshape(PAIR_COLS // 128, 2, 128).transpose(1, 0, 2)
     return result.reshape(1, 1, 2, PAIR_COLS)
 
 

time: 94.7 us -> 88.6 us (0.936)
  Pallas kernels: 38.1 us -> 30.1 us
  local copies, waits for them, and re-layouts: 0.01 us -> 1.85 us
    pallas_call x1 -> x0, Pallas kernels: 4.66 us -> none  [natural(): pl.pallas_call(natural_kernel, out_shape=jax.ShapeDtypeStruct((ROWS, 128)...]
    pallas_call x1, Pallas kernels: 32 us -> 28.6 us  [green_pairs(): pl.pallas_call(green_kernel, out_shape=jax.ShapeDtypeStruct((ROWS, 128),...]
    reshape x0 -> x1, local copies, waits for them, and re-layouts: none -> 1.76 us  [body(): return result.reshape(1, 1, 2, PAIR_COLS)]
where the time goes in v3:
time: 88.6 us; the launch traced here: 88.3 us
  blocking collectives  56.4 us (64%)
  Pallas kernels  30.1 us (34%)
  local copies, waits for them, and re-layouts  1.85 us (2%)
    all_to_all x2, blocking collectives, exchange(): lax.all_to_all(parts, ('energy', 'momentum'), split_axis=0, concat_axis=0...  56.4 us
    pallas_call x1, Pallas kernels, green_pairs(): pl.pallas_call(green_kernel, out_shape=jax.ShapeDtypeStruct((ROWS, 128),...  28.6 us

profile of v3, /device:TPU:1, one launch (start us, length us, event | category | flops | bytes accessed | tf_op | source)
XLA Modules:
  0.0 88.3 jit_solution(740855247370731054)
XLA Ops:
  0.0 28.6 %green_pairs.1 = f32[2304,128]{1,0:T(8,128)} custom-call(f32[1]{0:T(128)} %bitcast.energy_ref, s32[48,96]{1,0:T(8,128)} %bitcast.24, f32[2,384]{1,0:T(2,128)} %onsite_ref.1, f32[2304,128]{1,0:T(8,128)} %bitcast.22, f32[4,384,384]{2,1,0:T(8,128)} %bitcast.21, f32[2,384,384]{2,1,0:T(8,128)} %bitcast.23), custom_call_target="tpu_custom_call" | custom-call | tf_op jit(solution)/shard_map/green_pairs/pallas_call | solution.py:381
  28.6 0.0 copy-start
  28.7 0.0 copy-start.1
  28.7 31.8 %all_to_all.10 = f32[128,9,2,128]{3,2,1,0:T(2,128)S(1)} all-to-all(f32[128,9,2,128]{3,2,1,0:T(2,128)} %bitcast.20), channel_id=1, replica_groups=mesh['energy'=16,'momentum'=8] {'energy','momentum'}, dimensions={0} | all-to-all | bytes 2359296 | tf_op jit(solution)/shard_map/all_to_all | solution.py:465
  60.5 0.0 copy-done
  60.5 0.0 copy-done.1
  60.5 1.4 %convolve.1 = f32[2304,128]{1,0:T(8,128)S(1)} custom-call(s32[6]{0:T(128)S(1)} %copy-done.1, f32[6,2,8,8]{3,2,1,0:T(8,128)S(1)} %copy-done, f32[2304,128]{1,0:T(8,128)S(1)} %bitcast.16), custom_call_target="tpu_custom_call" | custom-call | tf_op jit(solution)/shard_map/convolve/pallas_call | solution.py:449
  61.9 24.6 %all_to_all.11 = f32[128,9,2,128]{3,2,1,0:T(2,128)S(1)} all-to-all(f32[128,9,2,128]{3,2,1,0:T(2,128)S(1)} %bitcast.17), channel_id=1, replica_groups=mesh['energy'=16,'momentum'=8] {'energy','momentum'}, dimensions={0} | all-to-all | bytes 2359296 | tf_op jit(solution)/shard_map/all_to_all | solution.py:465
  86.5 0.1 copy.11
  86.6 1.8 %reshape.35 = f32[1,1,2,147456]{3,2,1,0:T(2,128)} reshape(f32[2,1152,128]{2,1,0:T(8,128)S(1)} %bitcast.19) | data formatting | bytes 2359296 | tf_op jit(solution)/shard_map/reshape | solution.py:482
Async XLA Ops:
  28.6 31.8 %copy-start = (f32[6,2,8,8]{3,2,1,0:T(8,128)S(1)}, f32[6,2,8,8]{3,2,1,0:T(8,128)}, u32[]{:S(2)}) copy-start(f32[6,2,8,8]{3,2,1,0:T(8,128)} %phonon_ref.1) | copy-start | bytes 9220
  28.7 31.8 %copy-start.1 = (s32[6]{0:T(128)S(1)}, s32[6]{0:T(128)}, u32[]{:S(2)}) copy-start(s32[6]{0:T(128)} %shift_ref.1) | copy-start | bytes 76

commit v4 on v3

--- a/solution.py
+++ b/solution.py
@@ -16,6 +16,7 @@
 STRIP = 32
 DUO = 2 * ORB
 TILES = DUO // 128
+TOGETHER = 4
 GROUPS = ATOMS // 4
 
 F32 = jnp.float32
@@ -82,7 +83,7 @@
         order_ref[start : start + 64, :] = jnp.where(hot, 1.0, 0.0).astype(BF16)
 
 
-def place_group(shift_ref, sigma_ref, spread_ref, placed, group):
+def spread_group(shift_ref, sigma_ref, group):
     start = group * 96
     gap = jnp.zeros((16, 128), F32)
     cells = [sigma_ref[pl.ds(start + cell, 48, stride=2), :] for cell in range(2)]
@@ -129,14 +130,19 @@
     spread = lax.dot_general(
         jnp.concatenate(rows, axis=0), hot, (((1,), (1,)), ((), ())), preferred_element_type=F32
     )
-    spread_ref[...] = spread[0:256] + spread[256:512]
-    for j in range(4):
-        pieces = split(spread_ref[pl.ds(j, 64, stride=4), :])
-        for ref, piece in zip(placed, pieces):
-            for ct in range(4):
-                ref[pl.ds(pl.multiple_of(ORB * ct + 16 * group, 16), 16), 128 * j : 128 * (j + 1)] = piece[
-                    16 * ct : 16 * (ct + 1)
-                ]
+    return spread[0:256] + spread[256:512]
+
+
+def place_groups(shift_ref, sigma_ref, spread_ref, placed, first):
+    for k in range(TOGETHER):
+        spread_ref[k] = spread_group(shift_ref, sigma_ref, first + k)
+    for k in range(TOGETHER):
+        for j in range(4):
+            pieces = split(spread_ref[k, pl.ds(j, 64, stride=4), :])
+            for ref, piece in zip(placed, pieces):
+                for ct in range(4):
+                    rows = pl.ds(pl.multiple_of(ORB * ct + 16 * (first + k), 16), 16)
+                    ref[rows, 128 * j : 128 * (j + 1)] = piece[16 * ct : 16 * (ct + 1)]
 
 
 def assemble(placed, hop_ref, system, cell, t):
@@ -183,21 +189,22 @@
                     for i in range(4)
                 ]
             )
-        rows = pl.ds(ATOMS * v + start, 16)
+        rows = pl.ds(96 * (start // 32) + 32 * v + start % 32, 16)
         for i in range(4):
             value = jnp.concatenate([chosen_values[0][i], chosen_values[1][i]], axis=0)
             for ref, part in zip(picked, split(value)):
                 ref[rows, 128 * i : 128 * (i + 1)] = part
 
 
-def order_pairs(picked, order_ref, out_ref, cell):
-    value = jnp.dot(picked[0][...], order_ref[...], preferred_element_type=F32)
-    value = value + jnp.dot(picked[1][...], order_ref[...], preferred_element_type=F32)
+def order_pairs(picked, order_ref, out_ref, cell, chunk):
+    rows = slice(96 * chunk, 96 * (chunk + 1))
+    value = jnp.dot(picked[0][rows, :], order_ref[...], preferred_element_type=F32)
+    value = value + jnp.dot(picked[1][rows, :], order_ref[...], preferred_element_type=F32)
     for v in range(3):
-        for block in range(BLOCKS):
-            row = ATOMS * v + 8 * block
+        for block in range(4):
+            row = 32 * v + 8 * block
             for g in range(4):
-                to = (block * 8 * 12 + 4 * v + g) * 2 + cell
+                to = ((32 * chunk + 8 * block) * 12 + 4 * v + g) * 2 + cell
                 out_ref[pl.ds(to, 8, stride=24), :] = value[row : row + 8, 128 * g : 128 * (g + 1)]
 
 
@@ -243,9 +250,11 @@
     energy_ref,
     shift_ref,
     onsite_ref,
-    sigma_ref,
+    sigma_in_ref,
     hop_in_ref,
     coup_in_ref,
+    out_to_ref,
+    sigma_ref,
     out_ref,
     table_ref,
     order_ref,
@@ -271,6 +280,8 @@
     left_a, left_b, left_v, left_u, right_a, right_b, right_v = duos
     hop_copy = pltpu.make_async_copy(hop_in_ref, hop_ref, sems.at[0])
     coup_copy = pltpu.make_async_copy(coup_in_ref, coup_ref, sems.at[1])
+    sigma_copy = pltpu.make_async_copy(sigma_in_ref, sigma_ref, sems.at[2])
+    sigma_copy.start()
     hop_copy.start()
     coup_copy.start()
     energy = energy_ref[0]
@@ -279,11 +290,13 @@
     fill_tables(shift_ref, table_ref)
     fill_order(order_ref)
 
-    def place(group, carry):
-        place_group(shift_ref, sigma_ref, spread_ref, placed, group)
+    sigma_copy.wait()
+
+    def place(step, carry):
+        place_groups(shift_ref, sigma_ref, spread_ref, placed, step * TOGETHER)
         return carry
 
-    lax.fori_loop(0, GROUPS, place, 0, unroll=2)
+    lax.fori_loop(0, GROUPS // TOGETHER, place, 0)
     hop_copy.wait()
     coup_copy.wait()
     for t in range(2):
@@ -349,6 +362,10 @@
             pick_atoms(first_system, table_ref, second_picked, 32 * step + 16 * half)
 
     product(left_u, right_v, lambda tile, value: to_left(left_a, tile, split(value)), pick_second)
+    def send(chunk):
+        rows = slice(768 * chunk, 768 * (chunk + 1))
+        return pltpu.make_async_copy(out_ref.at[rows], out_to_ref.at[rows], sems.at[3 + chunk])
+
     for chunk in range(3):
         rows = slice(128 * chunk, 128 * (chunk + 1))
 
@@ -356,15 +373,23 @@
             green[tile, rows, :] += value
 
         def beside(step, chunk=chunk):
-            if step == 0 and chunk == 0:
-                order_pairs(second_picked, order_ref, out_ref, 1)
-            if step < 2 and chunk > 0:
-                pick_atoms(green, table_ref, first_picked, 32 * (chunk - 1) + 16 * step)
+            if step == 0:
+                order_pairs(second_picked, order_ref, out_ref, 1, chunk)
+            if chunk > 0:
+                if step < 2:
+                    pick_atoms(green, table_ref, first_picked, 32 * (chunk - 1) + 16 * step)
+                else:
+                    order_pairs(first_picked, order_ref, out_ref, 0, chunk - 1)
 
         product(left_a, right_a, through, beside, rows)
+        if chunk > 0:
+            send(chunk - 1).start()
     for half in range(2):
         pick_atoms(green, table_ref, first_picked, 64 + 16 * half)
-    order_pairs(first_picked, order_ref, out_ref, 0)
+    order_pairs(first_picked, order_ref, out_ref, 0, 2)
+    send(2).start()
+    for chunk in range(3):
+        send(chunk).wait()
 
 
 def vmem():
@@ -381,12 +406,14 @@
     return pl.pallas_call(
         green_kernel,
         out_shape=jax.ShapeDtypeStruct((ROWS, 128), F32),
-        in_specs=[smem()] + [vmem()] * 3 + [pl.BlockSpec(memory_space=pl.ANY)] * 2,
-        out_specs=vmem(),
+        in_specs=[smem()] + [vmem()] * 2 + [pl.BlockSpec(memory_space=pl.ANY)] * 3,
+        out_specs=pl.BlockSpec(memory_space=pl.ANY),
         scratch_shapes=[
+            pltpu.VMEM((ROWS, 128), F32),
+            pltpu.VMEM((ROWS, 128), F32),
             pltpu.VMEM((3, ATOMS, 128), jnp.int32),
             pltpu.VMEM((512, 512), BF16),
-            pltpu.VMEM((256, 128), F32),
+            pltpu.VMEM((TOGETHER, 256, 128), F32),
             pltpu.VMEM((8, ORB), F32),
             pltpu.VMEM((2, ORB, 128), F32),
             pltpu.VMEM((4, ORB, ORB), F32),
@@ -398,7 +425,7 @@
             pltpu.VMEM((4 * ORB, 512), BF16),
             pltpu.VMEM((4 * ORB, 512), BF16),
             *([pltpu.VMEM((3 * ATOMS, 512), BF16)] * 4),
-            pltpu.SemaphoreType.DMA((2,)),
+            pltpu.SemaphoreType.DMA((6,)),
             *left,
             *left,
             *left,
@@ -460,10 +487,12 @@
     return sigma.reshape(2, PAIR_COLS // 128, 128).transpose(1, 0, 2).reshape(ROWS, 128)
 
 
-def exchange(rows):
-    parts = rows.reshape(128, 9, 2, 128)
-    moved = lax.all_to_all(parts, ("energy", "momentum"), split_axis=0, concat_axis=0, tiled=True)
-    return moved.reshape(ROWS, 128)
+def exchange(parts):
+    return lax.all_to_all(parts, ("energy", "momentum"), split_axis=0, concat_axis=0, tiled=True)
+
+
+def to_parts(rows):
+    return rows.reshape(128, 9, 2, 128)
 
 
 def body(hopping, coupling, onsite, sigma_in, neighbor_shift, mode_shift, phonon_kernel):
@@ -477,9 +506,10 @@
         hopping.reshape(4, ORB, ORB),
         coupling.reshape(2, ORB, ORB),
     )
-    convolved = convolve(mode_shift, phonon_kernel, exchange(pairs))
-    result = exchange(convolved).reshape(PAIR_COLS // 128, 2, 128).transpose(1, 0, 2)
-    return result.reshape(1, 1, 2, PAIR_COLS)
+    convolved = convolve(mode_shift, phonon_kernel, exchange(to_parts(pairs)).reshape(ROWS, 128))
+    parts = convolved.reshape(128, 9, 2, 128).transpose(2, 0, 1, 3)
+    moved = lax.all_to_all(parts, ("energy", "momentum"), split_axis=1, concat_axis=1, tiled=True)
+    return moved.reshape(1, 1, 2, PAIR_COLS)
 
 
 def solution(mesh):

time: 88.6 us -> 86 us (0.971)
  Pallas kernels: 30.1 us -> 28.3 us
    all_to_all x0 -> x1, blocking collectives: none -> 24.6 us  [body(): lax.all_to_all(parts, ('energy', 'momentum'), split_axis=1, concat_axis=1...]
    all_to_all x2 -> x1, blocking collectives: 56.4 us -> 31.8 us  [exchange(): lax.all_to_all(parts, ('energy', 'momentum'), split_axis=0, concat_axis=0...]
    reshape x1 -> x0, local copies, waits for them, and re-layouts: 1.76 us -> none  [body(): return result.reshape(1, 1, 2, PAIR_COLS)]
    pallas_call x1, Pallas kernels: 28.6 us -> 26.9 us  [green_pairs(): pl.pallas_call(green_kernel, out_shape=jax.ShapeDtypeStruct((ROWS, 128),...]
    unnamed x4 -> x5, local copies, waits for them, and re-layouts: 0.01 us -> 1.03 us
where the time goes in v4:
time: 86 us; the launch traced here: 85.7 us
  blocking collectives  56.4 us (66%)
  Pallas kernels  28.3 us (33%)
  local copies, waits for them, and re-layouts  1.03 us (1%)
    all_to_all x1, blocking collectives, exchange(): lax.all_to_all(parts, ('energy', 'momentum'), split_axis=0, concat_axis=0...  31.8 us
    pallas_call x1, Pallas kernels, green_pairs(): pl.pallas_call(green_kernel, out_shape=jax.ShapeDtypeStruct((ROWS, 128),...  26.9 us
    all_to_all x1, blocking collectives, body(): lax.all_to_all(parts, ('energy', 'momentum'), split_axis=1, concat_axis=1...  24.6 us

profile of v4, /device:TPU:1, one launch (start us, length us, event | category | flops | bytes accessed | tf_op | source)
XLA Modules:
  0.0 85.7 jit_solution(10617418514946646377)
XLA Ops:
  0.0 26.9 %green_pairs.1 = f32[2304,128]{1,0:T(8,128)} custom-call(f32[1]{0:T(128)} %bitcast.energy_ref, s32[48,96]{1,0:T(8,128)} %bitcast.22, f32[2,384]{1,0:T(2,128)} %onsite_ref.1, f32[2304,128]{1,0:T(8,128)} %bitcast.20, f32[4,384,384]{2,1,0:T(8,128)} %bitcast.19, f32[2,384,384]{2,1,0:T(8,128)} %bitcast.21), custom_call_target="tpu_custom_call" | custom-call | tf_op jit(solution)/shard_map/green_pairs/pallas_call | solution.py:406
  26.9 0.0 copy-start
  26.9 0.0 copy-start.1
  26.9 31.8 %all_to_all.10 = f32[128,9,2,128]{3,2,1,0:T(2,128)S(1)} all-to-all(f32[128,9,2,128]{3,2,1,0:T(2,128)} %bitcast.18), channel_id=1, replica_groups=mesh['energy'=16,'momentum'=8] {'energy','momentum'}, dimensions={0} | all-to-all | bytes 2359296 | tf_op jit(solution)/shard_map/all_to_all | solution.py:491
  58.7 0.0 copy-done
  58.7 0.0 copy-done.1
  58.7 1.4 %convolve.1 = f32[2304,128]{1,0:T(8,128)S(1)} custom-call(s32[6]{0:T(128)S(1)} %copy-done.1, f32[6,2,8,8]{3,2,1,0:T(8,128)S(1)} %copy-done, f32[2304,128]{1,0:T(8,128)S(1)} %bitcast.15), custom_call_target="tpu_custom_call" | custom-call | tf_op jit(solution)/shard_map/convolve/pallas_call | solution.py:476
  60.2 24.6 %all_to_all.11 = f32[2,128,9,128]{3,0,2,1:T(2,128)S(1)} all-to-all(f32[2,128,9,128]{3,0,2,1:T(2,128)S(1)} %bitcast.16), channel_id=1, replica_groups=mesh['energy'=16,'momentum'=8] {'energy','momentum'}, dimensions={1} | all-to-all | bytes 2359296 | tf_op jit(solution)/shard_map/all_to_all | solution.py:511
  84.7 1.0 %copy.14 = f32[1,1,2,147456]{3,2,1,0:T(2,128)} copy(f32[1,1,2,147456]{3,2,1,0:T(2,128)S(1)} %bitcast.17) | data formatting | bytes 2359296
Async XLA Ops:
  26.9 31.8 %copy-start = (f32[6,2,8,8]{3,2,1,0:T(8,128)S(1)}, f32[6,2,8,8]{3,2,1,0:T(8,128)}, u32[]{:S(2)}) copy-start(f32[6,2,8,8]{3,2,1,0:T(8,128)} %phonon_ref.1) | copy-start | bytes 9220
  26.9 31.8 %copy-start.1 = (s32[6]{0:T(128)S(1)}, s32[6]{0:T(128)}, u32[]{:S(2)}) copy-start(s32[6]{0:T(128)} %shift_ref.1) | copy-start | bytes 76

commit v5 on v4

--- a/solution.py
+++ b/solution.py
@@ -16,7 +16,7 @@
 STRIP = 32
 DUO = 2 * ORB
 TILES = DUO // 128
-TOGETHER = 4
+TOGETHER = 8
 GROUPS = ATOMS // 4
 
 F32 = jnp.float32

time: 86 us -> 85.1 us (0.990)
  Pallas kernels: 28.3 us -> 27.4 us
    pallas_call x1, Pallas kernels: 26.9 us -> 25.9 us  [green_pairs(): pl.pallas_call(green_kernel, out_shape=jax.ShapeDtypeStruct((ROWS, 128),...]
where the time goes in v5:
time: 85.1 us; the launch traced here: 84.8 us
  blocking collectives  56.4 us (66%)
  Pallas kernels  27.4 us (32%)
  local copies, waits for them, and re-layouts  1.03 us (1%)
    all_to_all x1, blocking collectives, exchange(): lax.all_to_all(parts, ('energy', 'momentum'), split_axis=0, concat_axis=0...  31.8 us
    pallas_call x1, Pallas kernels, green_pairs(): pl.pallas_call(green_kernel, out_shape=jax.ShapeDtypeStruct((ROWS, 128),...  25.9 us
    all_to_all x1, blocking collectives, body(): lax.all_to_all(parts, ('energy', 'momentum'), split_axis=1, concat_axis=1...  24.6 us

profile of v5, /device:TPU:1, one launch (start us, length us, event | category | flops | bytes accessed | tf_op | source)
XLA Modules:
  0.0 84.8 jit_solution(8225335423760079035)
XLA Ops:
  0.0 25.9 %green_pairs.1 = f32[2304,128]{1,0:T(8,128)} custom-call(f32[1]{0:T(128)} %bitcast.energy_ref, s32[48,96]{1,0:T(8,128)} %bitcast.22, f32[2,384]{1,0:T(2,128)} %onsite_ref.1, f32[2304,128]{1,0:T(8,128)} %bitcast.20, f32[4,384,384]{2,1,0:T(8,128)} %bitcast.19, f32[2,384,384]{2,1,0:T(8,128)} %bitcast.21), custom_call_target="tpu_custom_call" | custom-call | tf_op jit(solution)/shard_map/green_pairs/pallas_call | solution.py:406
  26.0 0.0 copy-start
  26.0 0.0 copy-start.1
  26.0 31.8 %all_to_all.10 = f32[128,9,2,128]{3,2,1,0:T(2,128)S(1)} all-to-all(f32[128,9,2,128]{3,2,1,0:T(2,128)} %bitcast.18), channel_id=1, replica_groups=mesh['energy'=16,'momentum'=8] {'energy','momentum'}, dimensions={0} | all-to-all | bytes 2359296 | tf_op jit(solution)/shard_map/all_to_all | solution.py:491
  57.8 0.0 copy-done
  57.8 0.0 copy-done.1
  57.8 1.4 %convolve.1 = f32[2304,128]{1,0:T(8,128)S(1)} custom-call(s32[6]{0:T(128)S(1)} %copy-done.1, f32[6,2,8,8]{3,2,1,0:T(8,128)S(1)} %copy-done, f32[2304,128]{1,0:T(8,128)S(1)} %bitcast.15), custom_call_target="tpu_custom_call" | custom-call | tf_op jit(solution)/shard_map/convolve/pallas_call | solution.py:476
  59.2 24.6 %all_to_all.11 = f32[2,128,9,128]{3,0,2,1:T(2,128)S(1)} all-to-all(f32[2,128,9,128]{3,0,2,1:T(2,128)S(1)} %bitcast.16), channel_id=1, replica_groups=mesh['energy'=16,'momentum'=8] {'energy','momentum'}, dimensions={1} | all-to-all | bytes 2359296 | tf_op jit(solution)/shard_map/all_to_all | solution.py:511
  83.8 1.0 %copy.14 = f32[1,1,2,147456]{3,2,1,0:T(2,128)} copy(f32[1,1,2,147456]{3,2,1,0:T(2,128)S(1)} %bitcast.17) | data formatting | bytes 2359296
Async XLA Ops:
  26.0 31.8 %copy-start = (f32[6,2,8,8]{3,2,1,0:T(8,128)S(1)}, f32[6,2,8,8]{3,2,1,0:T(8,128)}, u32[]{:S(2)}) copy-start(f32[6,2,8,8]{3,2,1,0:T(8,128)} %phonon_ref.1) | copy-start | bytes 9220
  26.0 31.8 %copy-start.1 = (s32[6]{0:T(128)S(1)}, s32[6]{0:T(128)}, u32[]{:S(2)}) copy-start(s32[6]{0:T(128)} %shift_ref.1) | copy-start | bytes 76

commit v6 on v5

--- a/solution.py
+++ b/solution.py
@@ -16,7 +16,7 @@
 STRIP = 32
 DUO = 2 * ORB
 TILES = DUO // 128
-TOGETHER = 8
+TOGETHER = 24
 GROUPS = ATOMS // 4
 
 F32 = jnp.float32
@@ -83,13 +83,7 @@
         order_ref[start : start + 64, :] = jnp.where(hot, 1.0, 0.0).astype(BF16)
 
 
-def spread_group(shift_ref, sigma_ref, group):
-    start = group * 96
-    gap = jnp.zeros((16, 128), F32)
-    cells = [sigma_ref[pl.ds(start + cell, 48, stride=2), :] for cell in range(2)]
-    values = jnp.concatenate([cells[0], gap, cells[1], gap], axis=0).T
-    swapped = pltpu.roll(values, 64, 1)
-    lane32 = lax.broadcasted_iota(jnp.int32, (32, 128), 1)
+def fill_hot(shift_ref, hot_ref, group):
     lane = lax.broadcasted_iota(jnp.int32, (NEIGH, 128), 1)
     n = lax.broadcasted_iota(jnp.int32, (NEIGH, 128), 0)
     inner = lane % 64
@@ -99,50 +93,52 @@
     col = shift + atom
     col = jnp.where(col >= ATOMS, col - ATOMS, col).astype(F32)
     column = lax.broadcasted_iota(jnp.int32, (128, 128), 0).astype(F32)
-    hot = []
     for duo in range(2):
         mine = n == 4 * (inner % 12) + 2 * duo + lane // 64
         chosen = jnp.sum(jnp.where(mine, col, 0.0), axis=0, keepdims=True)
         chosen = jnp.where(inner[0:1] < 48, chosen, -1.0)
-        hot.append(jnp.where(column == chosen, 1.0, 0.0).astype(BF16))
-    hot = jnp.concatenate(hot, axis=1)
+        hot_ref[group, :, 128 * duo : 128 * (duo + 1)] = jnp.where(column == chosen, 1.0, 0.0).astype(BF16)
+
+
+def spread_groups(sigma_ref, hot_ref, cell, first):
+    gap = jnp.zeros((16, 128), F32)
+    groups = [sigma_ref[pl.ds((first + k) * 96 + cell, 48, stride=2), :] for k in range(2)]
+    values = jnp.concatenate([groups[0], gap, groups[1], gap], axis=0).T
+    swapped = pltpu.roll(values, 64, 1)
+    lane32 = lax.broadcasted_iota(jnp.int32, (32, 128), 1)
     inner16 = lax.broadcasted_iota(jnp.int32, (16, 128), 1) % 64
     kept = [jnp.where(inner16 // 12 == a, 1.0, 0.0).astype(BF16) for a in range(4)]
-    parts = []
-    for cell in range(2):
-        near, far = (values, swapped) if cell == 0 else (swapped, values)
-        parts.append(
-            [
-                split(jnp.where(lane32 < 64, near[64 * duo : 64 * duo + 32], far[64 * duo + 32 : 64 * duo + 64]))
-                for duo in range(2)
-            ]
+    out = []
+    for k in range(2):
+        near, far = (values, swapped) if k == 0 else (swapped, values)
+        parts = [
+            split(jnp.where(lane32 < 64, near[64 * duo : 64 * duo + 32], far[64 * duo + 32 : 64 * duo + 64]))
+            for duo in range(2)
+        ]
+        rows = [
+            jnp.concatenate([parts[duo][part][16 * t : 16 * (t + 1)] * kept[a] for duo in range(2)], axis=1)
+            for part in range(2)
+            for t in range(2)
+            for a in range(4)
+        ]
+        spread = lax.dot_general(
+            jnp.concatenate(rows, axis=0), hot_ref[first + k], (((1,), (1,)), ((), ())), preferred_element_type=F32
         )
-    rows = []
-    for part in range(2):
-        for cell in range(2):
-            for t in range(2):
-                for a in range(4):
-                    rows.append(
-                        jnp.concatenate(
-                            [parts[cell][duo][part][16 * t : 16 * (t + 1)] * kept[a] for duo in range(2)], axis=1
-                        )
-                    )
-    spread = lax.dot_general(
-        jnp.concatenate(rows, axis=0), hot, (((1,), (1,)), ((), ())), preferred_element_type=F32
-    )
-    return spread[0:256] + spread[256:512]
-
-
-def place_groups(shift_ref, sigma_ref, spread_ref, placed, first):
-    for k in range(TOGETHER):
-        spread_ref[k] = spread_group(shift_ref, sigma_ref, first + k)
-    for k in range(TOGETHER):
+        out.append(spread[0:128] + spread[128:256])
+    return out
+
+
+def place_groups(sigma_ref, hot_ref, spread_ref, placed, cell, first, count):
+    for k in range(0, count, 2):
+        for h, value in enumerate(spread_groups(sigma_ref, hot_ref, cell, first + k)):
+            spread_ref[k + h] = value
+    for k in range(count):
         for j in range(4):
-            pieces = split(spread_ref[k, pl.ds(j, 64, stride=4), :])
+            pieces = split(spread_ref[k, pl.ds(j, 32, stride=4), :])
             for ref, piece in zip(placed, pieces):
-                for ct in range(4):
-                    rows = pl.ds(pl.multiple_of(ORB * ct + 16 * (first + k), 16), 16)
-                    ref[rows, 128 * j : 128 * (j + 1)] = piece[16 * ct : 16 * (ct + 1)]
+                for t in range(2):
+                    rows = pl.ds(pl.multiple_of(ORB * (2 * cell + t) + 16 * (first + k), 16), 16)
+                    ref[rows, 128 * j : 128 * (j + 1)] = piece[16 * t : 16 * (t + 1)]
 
 
 def assemble(placed, hop_ref, system, cell, t):
@@ -258,6 +254,7 @@
     out_ref,
     table_ref,
     order_ref,
+    hot_ref,
     spread_ref,
     row_ref,
     col_ref,
@@ -293,7 +290,9 @@
     sigma_copy.wait()
 
     def place(step, carry):
-        place_groups(shift_ref, sigma_ref, spread_ref, placed, step * TOGETHER)
+        for k in range(TOGETHER):
+            fill_hot(shift_ref, hot_ref, step * TOGETHER + k)
+        place_groups(sigma_ref, hot_ref, spread_ref, placed, 0, step * TOGETHER, TOGETHER)
         return carry
 
     lax.fori_loop(0, GROUPS // TOGETHER, place, 0)
@@ -302,12 +301,11 @@
     for t in range(2):
         assemble(placed, hop_ref, first_system, 0, t)
     inverse_diagonal(energy, onsite_ref, 0, first_system, row_ref, col_ref)
-    for t in range(2):
-        assemble(placed, hop_ref, second_system, 1, t)
-        for strip in range(6 * t, 6 * t + 6):
-            scale_strip(first_system, row_ref, col_ref, base, left_a, right_a, strip * STRIP)
+    for strip in range(12):
+        scale_strip(first_system, row_ref, col_ref, base, left_a, right_a, strip * STRIP)
 
     def coupling(step):
+        place_groups(sigma_ref, hot_ref, spread_ref, placed, 1, 4 * step, 4)
         if step == 2:
             return
         turned = coup_ref[step].T
@@ -328,14 +326,23 @@
         to_right(right_b, tile, parts)
 
     product(left_a, right_a, second_term, coupling)
-    product(left_b, right_a, first_green)
+    product(
+        left_b,
+        right_a,
+        first_green,
+        lambda step: place_groups(sigma_ref, hot_ref, spread_ref, placed, 1, 12 + 4 * step, 4),
+    )
 
     def adjoint(tile, value):
         parts = split(value)
         to_left(left_b, tile, parts)
         to_right(right_a, tile, parts)
 
-    product(left_v, right_b, adjoint)
+    def second_assembled(step):
+        if step < 2:
+            assemble(placed, hop_ref, second_system, 1, step)
+
+    product(left_v, right_b, adjoint, second_assembled)
 
     def fold(tile, value):
         second_system[tile] -= value
@@ -413,7 +420,8 @@
             pltpu.VMEM((ROWS, 128), F32),
             pltpu.VMEM((3, ATOMS, 128), jnp.int32),
             pltpu.VMEM((512, 512), BF16),
-            pltpu.VMEM((TOGETHER, 256, 128), F32),
+            pltpu.VMEM((GROUPS, 128, 256), BF16),
+            pltpu.VMEM((TOGETHER, 128, 128), F32),
             pltpu.VMEM((8, ORB), F32),
             pltpu.VMEM((2, ORB, 128), F32),
             pltpu.VMEM((4, ORB, ORB), F32),

time: 85.1 us -> 84.5 us (level)
  no operation moved by 1% of the time
where the time goes in v6:
time: 84.5 us; the launch traced here: 84.3 us
  blocking collectives  56.4 us (67%)
  Pallas kernels  26.8 us (32%)
  local copies, waits for them, and re-layouts  1.03 us (1%)
    all_to_all x1, blocking collectives, exchange(): lax.all_to_all(parts, ('energy', 'momentum'), split_axis=0, concat_axis=0...  31.8 us
    pallas_call x1, Pallas kernels, green_pairs(): pl.pallas_call(green_kernel, out_shape=jax.ShapeDtypeStruct((ROWS, 128),...  25.4 us
    all_to_all x1, blocking collectives, body(): lax.all_to_all(parts, ('energy', 'momentum'), split_axis=1, concat_axis=1...  24.6 us

profile of v6, /device:TPU:1, one launch (start us, length us, event | category | flops | bytes accessed | tf_op | source)
XLA Modules:
  0.0 84.3 jit_solution(11097365051540981445)
XLA Ops:
  0.0 25.4 %green_pairs.1 = f32[2304,128]{1,0:T(8,128)} custom-call(f32[1]{0:T(128)} %bitcast.energy_ref, s32[48,96]{1,0:T(8,128)} %bitcast.22, f32[2,384]{1,0:T(2,128)} %onsite_ref.1, f32[2304,128]{1,0:T(8,128)} %bitcast.20, f32[4,384,384]{2,1,0:T(8,128)} %bitcast.19, f32[2,384,384]{2,1,0:T(8,128)} %bitcast.21), custom_call_target="tpu_custom_call" | custom-call | tf_op jit(solution)/shard_map/green_pairs/pallas_call | solution.py:413
  25.4 0.0 copy-start
  25.4 0.0 copy-start.1
  25.4 31.8 %all_to_all.10 = f32[128,9,2,128]{3,2,1,0:T(2,128)S(1)} all-to-all(f32[128,9,2,128]{3,2,1,0:T(2,128)} %bitcast.18), channel_id=1, replica_groups=mesh['energy'=16,'momentum'=8] {'energy','momentum'}, dimensions={0} | all-to-all | bytes 2359296 | tf_op jit(solution)/shard_map/all_to_all | solution.py:499
  57.2 0.0 copy-done
  57.3 0.0 copy-done.1
  57.3 1.4 %convolve.1 = f32[2304,128]{1,0:T(8,128)S(1)} custom-call(s32[6]{0:T(128)S(1)} %copy-done.1, f32[6,2,8,8]{3,2,1,0:T(8,128)S(1)} %copy-done, f32[2304,128]{1,0:T(8,128)S(1)} %bitcast.15), custom_call_target="tpu_custom_call" | custom-call | tf_op jit(solution)/shard_map/convolve/pallas_call | solution.py:484
  58.7 24.6 %all_to_all.11 = f32[2,128,9,128]{3,0,2,1:T(2,128)S(1)} all-to-all(f32[2,128,9,128]{3,0,2,1:T(2,128)S(1)} %bitcast.16), channel_id=1, replica_groups=mesh['energy'=16,'momentum'=8] {'energy','momentum'}, dimensions={1} | all-to-all | bytes 2359296 | tf_op jit(solution)/shard_map/all_to_all | solution.py:519
  83.3 1.0 %copy.14 = f32[1,1,2,147456]{3,2,1,0:T(2,128)} copy(f32[1,1,2,147456]{3,2,1,0:T(2,128)S(1)} %bitcast.17) | data formatting | bytes 2359296
Async XLA Ops:
  25.4 31.8 %copy-start = (f32[6,2,8,8]{3,2,1,0:T(8,128)S(1)}, f32[6,2,8,8]{3,2,1,0:T(8,128)}, u32[]{:S(2)}) copy-start(f32[6,2,8,8]{3,2,1,0:T(8,128)} %phonon_ref.1) | copy-start | bytes 9220
  25.4 31.8 %copy-start.1 = (s32[6]{0:T(128)S(1)}, s32[6]{0:T(128)}, u32[]{:S(2)}) copy-start(s32[6]{0:T(128)} %shift_ref.1) | copy-start | bytes 76
